TPU v7x, 256 devices: a whole 4x4x8 slice. The times are simulated.
256 devices in a mesh: gy: 8 (over y, x_hi), gx: 32 (over z, x_lo, core).
Axes of the slice: x: 4 (x_hi: 2, x_lo: 2; x = x_hi * 2 + x_lo), y: 4, z: 8, core: 2. Of those that a mesh axis runs over, the one named last changes fastest.
Arguments:
- current: float32 [256, 1024, 128], P('gy', 'gx'), may hold values from 0.25 to 4
- recorded: float32 [4, 256, 1024, 128], P(None, 'gy', 'gx'), may hold values from 0.25 to 4
- psf_depth: float32 [4, 31], replicated, may hold values from 0.02 to 1
- psf_rows: float32 [4, 31], replicated, may hold values from 0.02 to 1
- psf_cols: float32 [4, 31], replicated, may hold values from 0.02 to 1
Outputs:
- updated: float32 [256, 1024, 128], P('gy', 'gx')
All inputs are finite; a program needn't handle non-finite values.
Results may differ from a plain program's by a relative error of at most 0.0001.
Values sent between devices are 32-bit elements; how exact they have to be, the bound alone decides.
A program may use at most 192 MiB of HBM per device.

v0:
```python
import jax
import jax.numpy as jnp
from jax import lax
from jax.sharding import PartitionSpec as P


def with_halo(cells, sides, width):
    for axis, dim in sides:
        count = lax.axis_size(axis)
        ends = count - 1
        head = lax.slice_in_dim(cells, 0, width, axis=dim)
        tail = lax.slice_in_dim(cells, cells.shape[dim] - width, cells.shape[dim], axis=dim)
        cells = jnp.concatenate(
            [
                lax.ppermute(tail, axis, [(i, (i + 1) % count) for i in range(ends)]),
                cells,
                lax.ppermute(head, axis, [((i + 1) % count, i) for i in range(ends)]),
            ],
            axis=dim,
        )
    return cells


def normalized(kernel):
    return kernel / jnp.sum(kernel, axis=-1, keepdims=True)


def taps_valid(padded, weights, dimension, length):
    result = None
    for k in range(weights.shape[1]):
        window_part = lax.slice_in_dim(padded, k, k + length, axis=dimension)
        term = weights[:, k].reshape((-1,) + (1,) * (padded.ndim - 1)) * window_part
        result = term if result is None else result + term
    return result


def convolve(volume, weights, dimension):
    radius = weights.shape[1] // 2
    padding = [(0, 0)] * volume.ndim
    padding[dimension] = (radius, radius)
    return taps_valid(jnp.pad(volume, padding), weights, dimension, volume.shape[dimension])


def row_pass(volume, weights):
    radius = weights.shape[1] // 2
    padded = with_halo(volume, (("gy", 1),), radius)
    return taps_valid(padded, weights, 1, volume.shape[1])


def column_pass(volume, weights):
    results = []
    for v in range(volume.shape[0]):
        pencil = lax.all_to_all(volume[v], "gx", split_axis=0, concat_axis=1, tiled=True)
        convolved = convolve(pencil[None], weights[v : v + 1], 2)[0]
        results.append(lax.all_to_all(convolved, "gx", split_axis=1, concat_axis=0, tiled=True))
    outcome = jnp.stack(results)
    return outcome


def body(current, recorded, psf_depth, psf_rows, psf_cols):
    depth_taps = normalized(psf_depth)
    row_taps = normalized(psf_rows)
    col_taps = normalized(psf_cols)
    count = recorded.shape[0]
    blurred = column_pass(row_pass(convolve(current[None], depth_taps, 3), row_taps), col_taps)
    quotient = recorded / blurred
    backed = convolve(
        row_pass(column_pass(quotient, col_taps[:, ::-1]), row_taps[:, ::-1]),
        depth_taps[:, ::-1],
        3,
    )
    updated = current * (jnp.sum(backed, axis=0) / count)
    return updated


def solution(mesh):
    placed = (P("gy", "gx", None), P(None, "gy", "gx", None), P(), P(), P())
    return jax.shard_map(
        body, mesh=mesh, in_specs=placed, out_specs=P("gy", "gx", None), check_vma=False
    )
```

profile of v0, /device:TPU:1, one launch (start us, length us, event | category | flops | bytes accessed | tf_op | source)
XLA Modules:
  0.0 616.7 jit_solution(4121339849904252799)
XLA Ops:
  0.0 0.8 reduce_sum.36
  0.8 0.8 broadcast_divide_fusion.2
  2.4 12.0 %fusion.179 = (f32[32,32,128]{2,1,0:T(8,128)S(1)}, f32[32,32,128]{2,1,0:T(8,128)}, f32[32,32,128]{2,1,0:T(8,128)}, f32[32,32,128]{2,1,0:T(8,128)}, f32[32,32,128...) fusion(f32[1,32,32,128]{3,2,1,0:T(8,128)} %bitcast.233), kind=kLoop, calls=%fused_computation.332 | loop fusion | bytes 10485760 | tf_op jit(solution)/shard_map/mul | solution.py:32
  14.4 4.0 fusion.198
  18.5 10.4 %multiply_add_fusion = f32[4,32,32,128]{3,2,1,0:T(8,128)S(1)} fusion(f32[32,32,128]{2,1,0:T(8,128)} %get-tuple-element.110, f32[32,32,128]{2,1,0:T(8,128)} %get-tuple-element.109, f32[4]{0:T(128)S(1)} %get-tuple-element.37, f32[32,32,128]{2,1,0:T(8,128)} %get-tuple-element.108, f32[4]{0:T(128)S(1)} %get-tuple-element.38, ...), kind=kLoop, calls=%fused_computation.330 | loop fusion | flops 31981568 | bytes 18350576 | tf_op jit(solution)/shard_map/add | solution.py:33
  28.9 1.5 fusion.378
  30.4 6.4 %collective-permute-start = (f32[4,15,32,128]{3,2,1,0:T(8,128)}, f32[4,15,32,128]{3,2,1,0:T(8,128)}, u32[]{:S(2)}, u32[]{:S(2)}) collective-permute-start(f32[4,15,32,128]{3,2,1,0:T(8,128)} %get-tuple-element.79), channel_id=1, source_target_pairs={{0,32},{32,64},{64,96},{96,128},{128,160},{160,192},{192,224},{1,3... | collective-permute-start | bytes 2949128 | tf_op jit(solution)/shard_map/ppermute | solution.py:15
  36.8 1.7 collective-permute-start.1
  39.6 16.9 %collective-permute-done = f32[4,15,32,128]{3,2,1,0:T(8,128)} collective-permute-done((f32[4,15,32,128]{3,2,1,0:T(8,128)}, f32[4,15,32,128]{3,2,1,0:T(8,128)}, u32[]{:S(2)}, u32[]{:S(2)}) %collective-permute-start) | collective-permute-done | bytes 983072 | tf_op jit(solution)/shard_map/ppermute | solution.py:15
  56.6 23.0 %collective-permute-done.1 = f32[4,15,32,128]{3,2,1,0:T(8,128)} collective-permute-done((f32[4,15,32,128]{3,2,1,0:T(8,128)}, f32[4,15,32,128]{3,2,1,0:T(8,128)}, u32[]{:S(2)}, u32[]{:S(2)}) %collective-permute-start.1) | collective-permute-done | bytes 983072 | tf_op jit(solution)/shard_map/ppermute | solution.py:17
  79.6 14.6 %fusion.3 = f32[4,32,32,128]{3,2,1,0:T(8,128)S(1)} fusion(f32[4,32,32,128]{3,2,1,0:T(8,128)S(1)} %multiply_add_fusion, f32[4,15,32,128]{3,2,1,0:T(8,128)} %collective-permute-done.1, f32[4,15,32,128]{3,2,1,0:T(8,128)} %collective-permute-done, f32[4]{0:T(128)S(1)} %get-tuple-element.6, f32[4]{0:T(128)S(1)} %get-tuple-element.7, f32[4]{0:T(128)S(1)} %get-tuple-element.8, ...), kind=kLoop, calls=%fused_computation.121 | loop fusion | flops 47710208 | bytes 6160880 | tf_op jit(solution)/shard_map/add | solution.py:33
  94.3 1.0 slice_bitcast_fusion.7
  95.2 27.7 %all_to_all.168 = f32[32,32,128]{2,1,0:T(8,128)S(1)} all-to-all(f32[32,32,128]{2,1,0:T(8,128)S(1)} %get-tuple-element.78), channel_id=1, replica_groups=mesh['gy'=8,'gx'=32] {'gx'}, dimensions={0} | all-to-all | bytes 1048576 | tf_op jit(solution)/shard_map/all_to_all | solution.py:53
  123.0 21.2 %all_to_all.169 = f32[32,32,128]{2,1,0:T(8,128)S(1)} all-to-all(f32[32,32,128]{2,1,0:T(8,128)S(1)} %get-tuple-element.77), channel_id=1, replica_groups=mesh['gy'=8,'gx'=32] {'gx'}, dimensions={0} | all-to-all | bytes 1048576 | tf_op jit(solution)/shard_map/all_to_all | solution.py:53
  144.2 21.7 %all_to_all.170 = f32[32,32,128]{2,1,0:T(8,128)} all-to-all(f32[32,32,128]{2,1,0:T(8,128)S(1)} %get-tuple-element.75), channel_id=1, replica_groups=mesh['gy'=8,'gx'=32] {'gx'}, dimensions={0} | all-to-all | bytes 1048576 | tf_op jit(solution)/shard_map/all_to_all | solution.py:53
  165.9 4.8 all-to-all-start.6
  171.7 0.7 fusion.383
  173.1 22.0 %multiply_add_fusion.7 = f32[1,1,1024,128]{3,2,1,0:T(8,128)} fusion(f32[1,1,1024,128]{3,2,1,0:T(8,128)S(1)} %bitcast.255, f32[]{:T(128)} %bitcast.98, f32[]{:T(128)} %bitcast.97, f32[]{:T(128)} %bitcast.96, f32[]{:T(128)} %bitcast.95, f32[]{:T(128)} %bitcast.94, f32[]{:T(128)} %bitcast.93, f32[]{:T(128)} %bitcast.92, f32[]{:T(128)} %bitcast.91, ...), kind=kLoop, calls=%fused_computation.569 | loop fusion | flops 7995392 | bytes 1048700 | tf_op jit(solution)/shard_map/add | solution.py:33
  195.1 8.4 %all-to-all-start.3 = ((f32[1,1024,128]{2,0,1:T(1,128)}), f32[1,1024,128]{2,0,1:T(1,128)S(1)}, u32[]{:S(2)}, u32[]{:S(2)}) async-start(f32[1,1024,128]{2,0,1:T(1,128)} %bitcast.256), calls=%async_computation.3 | async-start | bytes 1048576 | tf_op jit(solution)/shard_map/all_to_all | solution.py:55
  203.5 0.7 fusion.381
  205.0 21.8 %multiply_add_fusion.6 = f32[1,1,1024,128]{3,2,1,0:T(8,128)} fusion(f32[1,1,1024,128]{3,2,1,0:T(8,128)S(1)} %bitcast.252, f32[]{:T(128)} %bitcast.133, f32[]{:T(128)} %bitcast.132, f32[]{:T(128)} %bitcast.131, f32[]{:T(128)} %bitcast.130, f32[]{:T(128)} %bitcast.129, f32[]{:T(128)} %bitcast.128, f32[]{:T(128)} %bitcast.127, f32[]{:T(128)} %bitcast.126, ...), kind=kLoop, calls=%fused_computation.536 | loop fusion | flops 7995392 | bytes 1048700 | tf_op jit(solution)/shard_map/add | solution.py:33
  226.8 8.3 %all-to-all-start.5 = ((f32[1,1024,128]{2,0,1:T(1,128)}), f32[1,1024,128]{2,0,1:T(1,128)}, u32[]{:S(2)}, u32[]{:S(2)}) async-start(f32[1,1024,128]{2,0,1:T(1,128)} %bitcast.134), calls=%async_computation.5 | async-start | bytes 1048576 | tf_op jit(solution)/shard_map/all_to_all | solution.py:55
  236.5 31.2 %multiply_add_fusion.8 = f32[1,1,1024,128]{3,2,1,0:T(8,128)} fusion(f32[1,1,1024,128]{3,2,1,0:T(8,128)} %bitcast.250, f32[]{:T(128)} %bitcast.63, f32[]{:T(128)} %bitcast.62, f32[]{:T(128)} %bitcast.61, f32[]{:T(128)} %bitcast.60, f32[]{:T(128)} %bitcast.59, f32[]{:T(128)} %bitcast.58, f32[]{:T(128)} %bitcast.57, f32[]{:T(128)} %bitcast.56, f32[]{:T(128)} %bitcast.55, ...), kind=kLoop, calls=%fused_computation.602 | loop fusion | flops 7995392 | bytes 1048700 | tf_op jit(solution)/shard_map/add | solution.py:33
  267.8 8.7 %all-to-all-start.1 = ((f32[1,1024,128]{2,0,1:T(1,128)}), f32[1,1024,128]{2,0,1:T(1,128)}, u32[]{:S(2)}, u32[]{:S(2)}) async-start(f32[1,1024,128]{2,0,1:T(1,128)} %bitcast.259), calls=%async_computation.1 | async-start | bytes 1048576 | tf_op jit(solution)/shard_map/all_to_all | solution.py:55
  276.5 31.7 %multiply_add_fusion.5 = f32[1,1,1024,128]{3,2,1,0:T(8,128)} fusion(f32[1,1,1024,128]{3,2,1,0:T(8,128)} %bitcast.249, f32[]{:T(128)} %bitcast.168, f32[]{:T(128)} %bitcast.167, f32[]{:T(128)} %bitcast.166, f32[]{:T(128)} %bitcast.165, f32[]{:T(128)} %bitcast.164, f32[]{:T(128)} %bitcast.163, f32[]{:T(128)} %bitcast.162, f32[]{:T(128)} %bitcast.161, ...), kind=kLoop, calls=%fused_computation.503 | loop fusion | flops 7995392 | bytes 1048700 | tf_op jit(solution)/shard_map/add | solution.py:33
  308.2 25.0 %all_to_all.171 = f32[1,1024,128]{2,0,1:T(1,128)S(1)} all-to-all(f32[1,1024,128]{2,0,1:T(1,128)} %bitcast.260), channel_id=1, replica_groups=mesh['gy'=8,'gx'=32] {'gx'}, dimensions={1} | all-to-all | bytes 1048576 | tf_op jit(solution)/shard_map/all_to_all | solution.py:55
  333.2 1.7 maximum_divide_fusion
  334.9 1.0 slice_bitcast_fusion.3
  335.9 21.2 %all_to_all.172 = f32[32,32,128]{2,1,0:T(8,128)S(1)} all-to-all(f32[32,32,128]{2,1,0:T(8,128)S(1)} %get-tuple-element.74), channel_id=1, replica_groups=mesh['gy'=8,'gx'=32] {'gx'}, dimensions={0} | all-to-all | bytes 1048576 | tf_op jit(solution)/shard_map/all_to_all | solution.py:53
  357.1 20.8 %all_to_all.173 = f32[32,32,128]{2,1,0:T(8,128)S(1)} all-to-all(f32[32,32,128]{2,1,0:T(8,128)S(1)} %get-tuple-element.73), channel_id=1, replica_groups=mesh['gy'=8,'gx'=32] {'gx'}, dimensions={0} | all-to-all | bytes 1048576 | tf_op jit(solution)/shard_map/all_to_all | solution.py:53
  377.9 21.0 %all_to_all.174 = f32[32,32,128]{2,1,0:T(8,128)S(1)} all-to-all(f32[32,32,128]{2,1,0:T(8,128)S(1)} %get-tuple-element.71), channel_id=1, replica_groups=mesh['gy'=8,'gx'=32] {'gx'}, dimensions={0} | all-to-all | bytes 1048576 | tf_op jit(solution)/shard_map/all_to_all | solution.py:53
  398.9 5.1 all-to-all-start.14
  404.0 22.0 %multiply_add_fusion.3 = f32[1,1,1024,128]{3,2,1,0:T(8,128)} fusion(f32[1,1,1024,128]{3,2,1,0:T(8,128)S(1)} %bitcast.257, f32[]{:T(128)} %bitcast.98, f32[]{:T(128)} %bitcast.97, f32[]{:T(128)} %bitcast.96, f32[]{:T(128)} %bitcast.95, f32[]{:T(128)} %bitcast.94, f32[]{:T(128)} %bitcast.93, f32[]{:T(128)} %bitcast.92, f32[]{:T(128)} %bitcast.91, ...), kind=kLoop, calls=%fused_computation.437 | loop fusion | flops 7995392 | bytes 1048700 | tf_op jit(solution)/shard_map/add | solution.py:33
  426.0 8.4 %all-to-all-start.11 = ((f32[1,1024,128]{2,0,1:T(1,128)}), f32[1,1024,128]{2,0,1:T(1,128)S(1)}, u32[]{:S(2)}, u32[]{:S(2)}) async-start(f32[1,1024,128]{2,0,1:T(1,128)} %bitcast.179), calls=%async_computation.11 | async-start | bytes 1048576 | tf_op jit(solution)/shard_map/all_to_all | solution.py:55
  434.4 21.8 %multiply_add_fusion.2 = f32[1,1,1024,128]{3,2,1,0:T(8,128)} fusion(f32[1,1,1024,128]{3,2,1,0:T(8,128)S(1)} %bitcast.254, f32[]{:T(128)} %bitcast.133, f32[]{:T(128)} %bitcast.132, f32[]{:T(128)} %bitcast.131, f32[]{:T(128)} %bitcast.130, f32[]{:T(128)} %bitcast.129, f32[]{:T(128)} %bitcast.128, f32[]{:T(128)} %bitcast.127, f32[]{:T(128)} %bitcast.126, ...), kind=kLoop, calls=%fused_computation.404 | loop fusion | flops 7995392 | bytes 1048700 | tf_op jit(solution)/shard_map/add | solution.py:33
  456.2 8.3 %all-to-all-start.13 = ((f32[1,1024,128]{2,0,1:T(1,128)}), f32[1,1024,128]{2,0,1:T(1,128)S(1)}, u32[]{:S(2)}, u32[]{:S(2)}) async-start(f32[1,1024,128]{2,0,1:T(1,128)} %bitcast.184), calls=%async_computation.13 | async-start | bytes 1048576 | tf_op jit(solution)/shard_map/all_to_all | solution.py:55
  464.4 22.0 %multiply_add_fusion.4 = f32[1,1,1024,128]{3,2,1,0:T(8,128)} fusion(f32[1,1,1024,128]{3,2,1,0:T(8,128)S(1)} %bitcast.253, f32[]{:T(128)} %bitcast.63, f32[]{:T(128)} %bitcast.62, f32[]{:T(128)} %bitcast.61, f32[]{:T(128)} %bitcast.60, f32[]{:T(128)} %bitcast.59, f32[]{:T(128)} %bitcast.58, f32[]{:T(128)} %bitcast.57, f32[]{:T(128)} %bitcast.56, ...), kind=kLoop, calls=%fused_computation.470 | loop fusion | flops 7995392 | bytes 1048700 | tf_op jit(solution)/shard_map/add | solution.py:33
  486.4 8.3 %all-to-all-start.9 = ((f32[1,1024,128]{2,0,1:T(1,128)}), f32[1,1024,128]{2,0,1:T(1,128)S(1)}, u32[]{:S(2)}, u32[]{:S(2)}) async-start(f32[1,1024,128]{2,0,1:T(1,128)} %bitcast.174), calls=%async_computation.9 | async-start | bytes 1048576 | tf_op jit(solution)/shard_map/all_to_all | solution.py:55
  494.7 21.4 %multiply_add_fusion.1 = f32[1,1,1024,128]{3,2,1,0:T(8,128)S(1)} fusion(f32[1,1,1024,128]{3,2,1,0:T(8,128)S(1)} %bitcast.251, f32[]{:T(128)} %bitcast.168, f32[]{:T(128)} %bitcast.167, f32[]{:T(128)} %bitcast.166, f32[]{:T(128)} %bitcast.165, f32[]{:T(128)} %bitcast.164, f32[]{:T(128)} %bitcast.163, f32[]{:T(128)} %bitcast.162, f32[]{:T(128)} %bitcast.161, ...), kind=kLoop, calls=%fused_computation.371 | loop fusion | flops 7995392 | bytes 1048700 | tf_op jit(solution)/shard_map/add | solution.py:33
  516.1 24.8 %all_to_all.175 = f32[1,1024,128]{2,0,1:T(1,128)S(1)} all-to-all(f32[1,1024,128]{2,0,1:T(1,128)S(1)} %bitcast.258), channel_id=1, replica_groups=mesh['gy'=8,'gx'=32] {'gx'}, dimensions={1} | all-to-all | bytes 1048576 | tf_op jit(solution)/shard_map/all_to_all | solution.py:55
  541.3 4.4 collective-permute-start.2
  545.7 1.3 collective-permute-start.3
  547.0 18.1 %collective-permute-done.2 = f32[4,15,32,128]{3,2,1,0:T(8,128)S(1)} collective-permute-done((f32[4,15,32,128]{3,2,1,0:T(8,128)S(1)}, f32[4,15,32,128]{3,2,1,0:T(8,128)S(1)}, u32[]{:S(2)}, u32[]{:S(2)}) %collective-permute-start.2) | collective-permute-done | bytes 983072 | tf_op jit(solution)/shard_map/ppermute | solution.py:15
  565.1 23.3 %collective-permute-done.3 = f32[4,15,32,128]{3,2,1,0:T(8,128)S(1)} collective-permute-done((f32[4,15,32,128]{3,2,1,0:T(8,128)S(1)}, f32[4,15,32,128]{3,2,1,0:T(8,128)S(1)}, u32[]{:S(2)}, u32[]{:S(2)}) %collective-permute-start.3) | collective-permute-done | bytes 983072 | tf_op jit(solution)/shard_map/ppermute | solution.py:17
  588.5 0.9 maximum_maximum_fusion
  589.4 9.5 %fusion.146 = f32[4,32,32,128]{3,2,1,0:T(8,128)S(1)} fusion(f32[4,47,32,128]{3,2,1,0:T(8,128)S(1)} %get-tuple-element.68, f32[4,47,32,128]{3,2,1,0:T(8,128)S(1)} %get-tuple-element.67, f32[4]{0:T(128)S(1)} %get-tuple-element.6, f32[4]{0:T(128)S(1)} %get-tuple-element.7, f32[4]{0:T(128)S(1)} %get-tuple-element.8, f32[4]{0:T(128)S(1)} %get-tuple-element.9, ...), kind=kLoop, calls=%fused_computation.265 | loop fusion | flops 33554432 | bytes 67109360 | tf_op jit(solution)/shard_map/add | solution.py:33
  598.8 16.7 %fusion.178 = f32[32,32,128]{2,1,0:T(8,128)S(1)} fusion(f32[4,32,32,128]{3,2,1,0:T(8,128)S(1)} %fusion.146, f32[4]{0:T(128)S(1)} %get-tuple-element.37, f32[4]{0:T(128)S(1)} %get-tuple-element.38, f32[4]{0:T(128)S(1)} %get-tuple-element.39, f32[4]{0:T(128)S(1)} %get-tuple-element.40, f32[4]{0:T(128)S(1)} %get-tuple-element.41, f32[4]{0:T(128)S(1)} %get-tuple-element.42, ...), kind=kLoop, calls=%fused_computation.331 | loop fusion | flops 32374784 | bytes 2621936 | tf_op jit(solution)/shard_map/reduce_sum | solution.py:72
  615.6 0.9 multiply_multiply_fusion
  (33 shorter events, 6.2 us)
Async XLA Ops:
  2.4 12.0 %copy-start = (f32[32,32,128]{2,1,0:T(8,128)S(1)}, f32[32,32,128]{2,1,0:T(8,128)}, u32[]{:S(2)}) copy-start(f32[32,32,128]{2,1,0:T(8,128)} %param.5) | copy-start | bytes 1572868
  28.9 9.7 %copy-start.3 = (f32[4,31]{1,0:T(4,128)S(1)}, f32[4,31]{1,0:T(4,128)}, u32[]{:S(2)}) copy-start(f32[4,31]{1,0:T(4,128)} %param.8) | copy-start | bytes 1492
  30.4 26.2 %collective-permute-start = (f32[4,15,32,128]{3,2,1,0:T(8,128)}, f32[4,15,32,128]{3,2,1,0:T(8,128)}, u32[]{:S(2)}, u32[]{:S(2)}) collective-permute-start(f32[4,15,32,128]{3,2,1,0:T(8,128)} %get-tuple-element.79), channel_id=1, source_target_pairs={{0,32},{32,64},{64,96},{96,128},{128,160},{160,192},{192,224},{1,3... | collective-permute-start | bytes 2949128 | tf_op jit(solution)/shard_map/ppermute | solution.py:15
  36.8 42.8 %collective-permute-start.1 = (f32[4,15,32,128]{3,2,1,0:T(8,128)}, f32[4,15,32,128]{3,2,1,0:T(8,128)}, u32[]{:S(2)}, u32[]{:S(2)}) collective-permute-start(f32[4,15,32,128]{3,2,1,0:T(8,128)} %get-tuple-element.80), channel_id=1, source_target_pairs={{32,0},{64,32},{96,64},{128,96},{160,128},{192,160},{224,192},{33,... | collective-permute-start | bytes 2949128 | tf_op jit(solution)/shard_map/ppermute | solution.py:17
  95.2 75.5 %copy-start.4 = (f32[4,31]{1,0:T(4,128)S(1)}, f32[4,31]{1,0:T(4,128)}, u32[]{:S(2)}) copy-start(f32[4,31]{1,0:T(4,128)} %param.9) | copy-start | bytes 1492
  165.9 29.2 %all-to-all-start.6 = ((f32[32,32,128]{2,1,0:T(8,128)}), f32[32,32,128]{2,1,0:T(8,128)S(1)}, u32[]{:S(2)}, u32[]{:S(2)}) async-start(f32[32,32,128]{2,1,0:T(8,128)} %get-tuple-element.76), calls=%async_computation.6 | async-start | bytes 1048576 | tf_op jit(solution)/shard_map/all_to_all | solution.py:53
  195.1 41.4 %copy-start.2 = (f32[32,32,128]{2,1,0:T(8,128)}, f32[32,32,128]{2,1,0:T(8,128)S(1)}, u32[]{:S(2)}) copy-start(f32[32,32,128]{2,1,0:T(8,128)S(1)} %all-to-all-done.6) | copy-start | bytes 1572868
  195.1 31.6 %all-to-all-start.3 = ((f32[1,1024,128]{2,0,1:T(1,128)}), f32[1,1024,128]{2,0,1:T(1,128)S(1)}, u32[]{:S(2)}, u32[]{:S(2)}) async-start(f32[1,1024,128]{2,0,1:T(1,128)} %bitcast.256), calls=%async_computation.3 | async-start | bytes 1048576 | tf_op jit(solution)/shard_map/all_to_all | solution.py:55
  226.8 41.0 %all-to-all-start.5 = ((f32[1,1024,128]{2,0,1:T(1,128)}), f32[1,1024,128]{2,0,1:T(1,128)}, u32[]{:S(2)}, u32[]{:S(2)}) async-start(f32[1,1024,128]{2,0,1:T(1,128)} %bitcast.134), calls=%async_computation.5 | async-start | bytes 1048576 | tf_op jit(solution)/shard_map/all_to_all | solution.py:55
  236.5 96.7 %copy-start.1 = (f32[4,32,32,128]{3,2,1,0:T(8,128)S(1)}, f32[4,32,32,128]{3,2,1,0:T(8,128)}, u32[]{:S(2)}) copy-start(f32[4,32,32,128]{3,2,1,0:T(8,128)} %param.6) | copy-start | bytes 6291460
  267.8 40.4 %all-to-all-start.1 = ((f32[1,1024,128]{2,0,1:T(1,128)}), f32[1,1024,128]{2,0,1:T(1,128)}, u32[]{:S(2)}, u32[]{:S(2)}) async-start(f32[1,1024,128]{2,0,1:T(1,128)} %bitcast.259), calls=%async_computation.1 | async-start | bytes 1048576 | tf_op jit(solution)/shard_map/all_to_all | solution.py:55
  398.9 27.1 %all-to-all-start.14 = ((f32[32,32,128]{2,1,0:T(8,128)}), f32[32,32,128]{2,1,0:T(8,128)S(1)}, u32[]{:S(2)}, u32[]{:S(2)}) async-start(f32[32,32,128]{2,1,0:T(8,128)} %get-tuple-element.72), calls=%async_computation.14 | async-start | bytes 1048576 | tf_op jit(solution)/shard_map/all_to_all | solution.py:53
  426.0 30.2 %all-to-all-start.11 = ((f32[1,1024,128]{2,0,1:T(1,128)}), f32[1,1024,128]{2,0,1:T(1,128)S(1)}, u32[]{:S(2)}, u32[]{:S(2)}) async-start(f32[1,1024,128]{2,0,1:T(1,128)} %bitcast.179), calls=%async_computation.11 | async-start | bytes 1048576 | tf_op jit(solution)/shard_map/all_to_all | solution.py:55
  456.2 30.3 %all-to-all-start.13 = ((f32[1,1024,128]{2,0,1:T(1,128)}), f32[1,1024,128]{2,0,1:T(1,128)S(1)}, u32[]{:S(2)}, u32[]{:S(2)}) async-start(f32[1,1024,128]{2,0,1:T(1,128)} %bitcast.184), calls=%async_computation.13 | async-start | bytes 1048576 | tf_op jit(solution)/shard_map/all_to_all | solution.py:55
  486.4 29.7 %all-to-all-start.9 = ((f32[1,1024,128]{2,0,1:T(1,128)}), f32[1,1024,128]{2,0,1:T(1,128)S(1)}, u32[]{:S(2)}, u32[]{:S(2)}) async-start(f32[1,1024,128]{2,0,1:T(1,128)} %bitcast.174), calls=%async_computation.9 | async-start | bytes 1048576 | tf_op jit(solution)/shard_map/all_to_all | solution.py:55
  541.3 23.8 %collective-permute-start.2 = (f32[4,15,32,128]{3,2,1,0:T(8,128)S(1)}, f32[4,15,32,128]{3,2,1,0:T(8,128)S(1)}, u32[]{:S(2)}, u32[]{:S(2)}) collective-permute-start(f32[4,15,32,128]{3,2,1,0:T(8,128)S(1)} %get-tuple-element.69), channel_id=1, source_target_pairs={{0,32},{32,64},{64,96},{96,128},{128,160},{160,192},{192,224},{1,3... | collective-permute-start | bytes 2949128 | tf_op jit(solution)/shard_map/ppermute | solution.py:15
  545.7 42.7 %collective-permute-start.3 = (f32[4,15,32,128]{3,2,1,0:T(8,128)S(1)}, f32[4,15,32,128]{3,2,1,0:T(8,128)S(1)}, u32[]{:S(2)}, u32[]{:S(2)}) collective-permute-start(f32[4,15,32,128]{3,2,1,0:T(8,128)S(1)} %get-tuple-element.70), channel_id=1, source_target_pairs={{32,0},{64,32},{96,64},{128,96},{160,128},{192,160},{224,192},{33,... | collective-permute-start | bytes 2949128 | tf_op jit(solution)/shard_map/ppermute | solution.py:17
where the time goes:
time: 629 us; the launch traced here: 617 us
  other arithmetic  251 us (40%)
  blocking collectives  183 us (29%)
  waiting for transfers between devices  81.4 us (13%)
  starting transfers between devices  74.1 us (12%)
  local copies, waits for them, and re-layouts  26.5 us (4%)
    add x11, other arithmetic, taps_valid(): result = term if result is None else result + term  228 us
    all_to_all x6, blocking collectives, column_pass(): lax.all_to_all(volume[v], 'gx', split_axis=0, concat_axis=1, tiled=True)  134 us
    all_to_all x6, starting transfers between devices, column_pass(): lax.all_to_all(convolved, 'gx', split_axis=1, concat_axis=0, tiled=True)  50.3 us
    all_to_all x2, blocking collectives, column_pass(): lax.all_to_all(convolved, 'gx', split_axis=1, concat_axis=0, tiled=True)  49.8 us
    ppermute x2, waiting for transfers between devices, with_halo(): lax.ppermute(head, axis, [((i + 1) % count, i) for i in range(ends)])  46.4 us
    ppermute x2, waiting for transfers between devices, with_halo(): lax.ppermute(tail, axis, [(i, (i + 1) % count) for i in range(ends)])  35 us
    reduce_sum x1, other arithmetic, body(): updated = current * (jnp.sum(backed, axis=0) / count)  16.7 us
    mul x2, local copies, waits for them, and re-layouts, taps_valid(): term = weights[:, k].reshape((-1,) + (1,) * (padded.ndim - 1)) * window_part  16 us
  transfers between devices with their start and end apart: 12, of which 4 were waited for; matrix products, arithmetic and copies ran while one was open for 32% of the time, Pallas kernels for 0%

commit v1 on v0

v1 whole, which is shorter than its diff:
```python
import functools

import jax
import jax.numpy as jnp
from jax import lax
from jax.experimental import pallas as pl
from jax.experimental.pallas import tpu as pltpu
from jax.sharding import PartitionSpec as P

F32 = jnp.float32
BF16 = jnp.bfloat16
TAPS = 31
RAD = 15
VIEWS = 4
B = 32
H = 16
ROWS = B + 2 * RAD
COLS = B + 2 * H
Z = 128


def split(x):
    hi = x.astype(BF16)
    return hi, (x - hi.astype(F32)).astype(BF16)


def triple_rows(x):
    hi, lo = split(x)
    return jnp.concatenate([hi, lo, hi], axis=0)


def triple_lanes(x):
    hi, lo = split(x)
    return jnp.concatenate([hi, lo, hi], axis=1)


def dot(a, b):
    return jnp.dot(a, b, preferred_element_type=F32)


def tap_sum(ref, v):
    total = ref[v, 0]
    for t in range(1, TAPS):
        total = total + ref[v, t]
    return total


def kernel(ny, nx, cur, rec, kz, ky, kx, out, u, xb, yb, rv, p, ry, rxp, rxo, rd, rpc,
           tf, tb, wf, wb, local_sem, send_sem, recv_sem):
    i = lax.axis_index("gy")
    j = lax.axis_index("gx")
    side = lax.rem(j, 2)
    up = lax.rem(i + ny - 1, ny)
    down = lax.rem(i + 1, ny)
    away = lax.rem(j + nx - 1 + 2 * side, nx)
    mate = j + 1 - 2 * side

    def col(x):
        return pl.ds(pl.multiple_of(x, H), H)

    own_away = H * side
    own_mate = H * (1 - side)
    halo_away = 48 * side
    halo_mate = 48 * (1 - side)

    load_rec = pltpu.make_async_copy(rec, rv, local_sem.at[0])
    load_cur = pltpu.make_async_copy(cur, u.at[pl.ds(RAD, B), pl.ds(H, B), :], local_sem.at[1])
    load_cur.start()
    load_rec.start()

    barrier = pltpu.get_barrier_semaphore()
    peers = [(up, j), (down, j), (i, away), (i, mate), (up, away), (down, away)]
    for peer in peers:
        pl.semaphore_signal(barrier, inc=1, device_id=peer, device_id_type=pl.DeviceIdType.MESH)
    pl.semaphore_wait(barrier, len(peers))

    def remote(k, src, dst, peer):
        return pltpu.make_async_remote_copy(
            src_ref=src, dst_ref=dst, send_sem=send_sem.at[k], recv_sem=recv_sem.at[k],
            device_id=peer, device_id_type=pl.DeviceIdType.MESH)

    top = pl.ds(0, RAD)
    bottom = pl.ds(RAD + B, RAD)
    mid = pl.ds(RAD, B)
    first = pl.ds(0, RAD)
    last = pl.ds(B - RAD, RAD)

    up_mate = remote(0, cur.at[first, col(own_mate), :], u.at[bottom, col(H + own_mate), :], (up, j))
    down_mate = remote(1, cur.at[last, col(own_mate), :], u.at[top, col(H + own_mate), :], (down, j))
    up_away = remote(2, cur.at[first, col(own_away), :], u.at[bottom, col(H + own_away), :], (up, j))
    down_away = remote(3, cur.at[last, col(own_away), :], u.at[top, col(H + own_away), :], (down, j))
    side_away = remote(4, cur.at[:, col(own_away), :], u.at[mid, col(48 - halo_away), :], (i, away))
    side_mate = remote(5, cur.at[:, col(own_mate), :], u.at[mid, col(48 - halo_mate), :], (i, mate))
    diag_up = remote(6, cur.at[first, col(own_away), :], u.at[bottom, col(48 - halo_away), :], (up, away))
    diag_down = remote(7, cur.at[last, col(own_away), :], u.at[top, col(48 - halo_away), :], (down, away))
    pass_top = remote(8, u.at[top, col(H + own_mate), :], u.at[top, col(48 - halo_mate), :], (i, mate))
    pass_bottom = remote(9, u.at[bottom, col(H + own_mate), :], u.at[bottom, col(48 - halo_mate), :], (i, mate))
    for c in (side_mate, side_away, up_mate, down_mate, up_away, down_away, diag_up, diag_down):
        c.start()

    row_id = lax.broadcasted_iota(jnp.int32, (B, Z), 0)
    lane_id = lax.broadcasted_iota(jnp.int32, (B, Z), 1)
    low = jnp.where(j == 0, H, 0)
    high = jnp.where(j == nx - 1, H + B, COLS)
    inside = (lane_id >= low) & (lane_id < high)
    parts = []
    for v in range(VIEWS):
        band = jnp.zeros((B, Z), F32)
        for t in range(TAPS):
            band = jnp.where(lane_id - row_id == t + 1, kx[v, t], band)
        band = band / jnp.full((B, Z), tap_sum(kx, v), F32)
        parts.append(jnp.where(inside, band, 0.0))
    full = jnp.concatenate(parts, axis=0)
    flipped = full.T[:COLS]
    keep_top = jnp.where(i == 0, 0.0, 1.0).astype(F32)
    keep_bottom = jnp.where(i == ny - 1, 0.0, 1.0).astype(F32)
    for n, keep in enumerate((None, keep_top, keep_bottom)):
        a = full if keep is None else full * keep
        b = flipped if keep is None else flipped * keep
        hi, lo = split(a[:, :COLS])
        tf[n, :, 0:COLS] = hi
        tf[n, :, COLS:2 * COLS] = hi
        tf[n, :, 2 * COLS:3 * COLS] = lo
        hi, lo = split(b)
        tb[n, :, 0:Z] = hi
        tb[n, :, Z:2 * Z] = hi
        tb[n, :, 2 * Z:3 * Z] = lo

    def depth_matrix(v, c):
        r = lax.broadcasted_iota(jnp.int32, (Z, Z), 0)
        l = lax.broadcasted_iota(jnp.int32, (Z, Z), 1)
        band = jnp.zeros((Z, Z), F32)
        for t in range(TAPS):
            band = jnp.where(r - l == t - RAD, kz[v, t], band)
        band = band / jnp.full((Z, Z), tap_sum(kz, v) * tap_sum(ky, v), F32)
        for ref, m in ((wf, band), (wb, band.T)):
            hi, lo = split(m)
            ref[v, 0:Z, :] = hi
            ref[v, Z:2 * Z, :] = hi
            ref[v, 2 * Z:3 * Z, :] = lo
        return c

    lax.fori_loop(0, VIEWS, depth_matrix, 0)

    def x_forward(start, count, n):
        data = jnp.concatenate([triple_rows(u[start + r]) for r in range(count)], axis=1)
        res = dot(tf[n], data)
        for r in range(count):
            xb[start + r] = res[:, r * Z:(r + 1) * Z]

    load_cur.wait()
    side_mate.wait_recv()
    side_away.wait_recv()

    def own_rows(g, c):
        x_forward(RAD + 4 * g, 4, 0)
        return c

    lax.fori_loop(0, B // 4, own_rows, 0)

    def y_forward_own(n, c):
        off = pl.ds(pl.multiple_of(n * 8, 8), 8)
        v = n // 4
        w = [ky[v, t] for t in range(TAPS)]
        for b in range(4):
            acc = [None] * 8
            for r in range(max(RAD, 8 * b), min(RAD + B - 1, 8 * b + 37) + 1):
                x = xb[r, off, :]
                for o in range(8):
                    t = r - (8 * b + o)
                    if 0 <= t < TAPS:
                        term = w[t] * x
                        acc[o] = term if acc[o] is None else acc[o] + term
            for o in range(8):
                yb[8 * b + o, off, :] = acc[o]
        return c

    lax.fori_loop(0, 16, y_forward_own, 0)

    down_mate.wait_recv()
    pass_top.start()
    up_mate.wait_recv()
    pass_bottom.start()
    down_away.wait_recv()
    up_away.wait_recv()
    diag_down.wait_recv()
    diag_up.wait_recv()
    pass_top.wait_recv()
    pass_bottom.wait_recv()

    def halo_rows(g, c):
        s = jnp.minimum(4 * g, RAD - 4)
        x_forward(s, 4, 1)
        x_forward(RAD + B + s, 4, 2)
        return c

    lax.fori_loop(0, 4, halo_rows, 0)

    def y_forward_halo(n, c):
        off = pl.ds(pl.multiple_of(n * 8, 8), 8)
        v = n // 4
        w = [ky[v, t] for t in range(TAPS)]
        for b in range(4):
            outs = [8 * b + o for o in range(8)]
            acc = {}
            for r in list(range(0, RAD)) + list(range(RAD + B, ROWS)):
                hits = [o for o in outs if 0 <= r - o < TAPS]
                if not hits:
                    continue
                x = xb[r, off, :]
                for o in hits:
                    term = w[r - o] * x
                    acc[o] = acc[o] + term if o in acc else term
            for o, a in acc.items():
                yb[o, off, :] += a
        return c

    lax.fori_loop(0, 16, y_forward_halo, 0)

    load_rec.wait()

    def depth(n, c):
        v = n // 4
        rows = pl.ds(pl.multiple_of(lax.rem(n, 4) * 8, 8), 8)
        lines = pl.ds(pl.multiple_of(v * B, B), B)
        blurred = dot(triple_lanes(yb[rows, lines, :].reshape(8 * B, Z)), wf[v])
        quotient = rv[v, rows].reshape(8 * B, Z) / blurred
        yb[rows, lines, :] = dot(triple_lanes(quotient), wb[v]).reshape(8, B, Z)
        return c

    lax.fori_loop(0, 16, depth, 0)

    def y_backward(rows):
        def step(n, c):
            off = pl.ds(pl.multiple_of(n * 8, 8), 8)
            v = n // 4
            w = [ky[v, t] for t in range(TAPS)]
            for group in rows:
                acc = {}
                for q in range(max(0, group[0] - TAPS + 1), min(B - 1, group[-1]) + 1):
                    x = yb[q, off, :]
                    for r in group:
                        if 0 <= r - q < TAPS:
                            term = w[r - q] * x
                            acc[r] = acc[r] + term if r in acc else term
                for r, a in acc.items():
                    xb[r, off, :] = a
            return c

        lax.fori_loop(0, 16, step, 0)

    def x_backward(start, count, n):
        data = jnp.concatenate([triple_rows(xb[start + r]) for r in range(count)], axis=1)
        res = dot(tb[n], data)
        for r in range(count):
            p[start + r] = res[:, r * Z:(r + 1) * Z]

    y_backward([range(0, 8), range(8, 15), range(47, 55), range(55, 62)])

    def halo_back(g, c):
        s = jnp.minimum(4 * g, RAD - 4)
        x_backward(s, 4, 1)
        x_backward(RAD + B + s, 4, 2)
        return c

    lax.fori_loop(0, 4, halo_back, 0)

    mate_top = remote(10, p.at[top, col(halo_mate), :], rpc.at[0], (i, mate))
    mate_bottom = remote(11, p.at[bottom, col(halo_mate), :], rpc.at[1], (i, mate))
    back_up_away = remote(12, p.at[top, col(H + own_away), :], ry.at[1, :, col(own_away), :], (up, j))
    back_down_away = remote(13, p.at[bottom, col(H + own_away), :], ry.at[0, :, col(own_away), :], (down, j))
    back_up_mate = remote(14, p.at[top, col(H + own_mate), :], ry.at[1, :, col(own_mate), :], (up, j))
    back_down_mate = remote(15, p.at[bottom, col(H + own_mate), :], ry.at[0, :, col(own_mate), :], (down, j))
    back_diag_up = remote(16, p.at[top, col(halo_away), :], rd.at[1], (up, away))
    back_diag_down = remote(17, p.at[bottom, col(halo_away), :], rd.at[0], (down, away))
    back_away = remote(18, p.at[mid, col(halo_away), :], rxo, (i, away))
    back_mate = remote(19, p.at[mid, col(halo_mate), :], rxp, (i, mate))
    mate_top.start()
    mate_bottom.start()
    back_up_away.start()
    back_down_away.start()
    mate_top.wait_recv()
    p[top, col(H + own_mate), :] += rpc[0]
    back_up_mate.start()
    mate_bottom.wait_recv()
    p[bottom, col(H + own_mate), :] += rpc[1]
    back_down_mate.start()
    back_diag_up.start()
    back_diag_down.start()

    y_backward([range(RAD + 8 * b, RAD + 8 * b + 8) for b in range(4)])

    def own_back(g, c):
        x_backward(RAD + 4 * g, 4, 0)
        return c

    lax.fori_loop(0, B // 4, own_back, 0)
    back_mate.start()
    back_away.start()

    back_mate.wait()
    p[mid, col(H + own_mate), :] += rxp[...]
    back_away.wait()
    p[mid, col(H + own_away), :] += rxo[...]
    back_diag_down.wait()
    p[pl.ds(RAD, RAD), col(H + own_away), :] += rd[0]
    back_diag_up.wait()
    p[pl.ds(B, RAD), col(H + own_away), :] += rd[1]
    for c in (back_down_away, back_down_mate, back_up_away, back_up_mate):
        c.wait()
    p[pl.ds(RAD, RAD), pl.ds(H, B), :] += ry[0]
    p[pl.ds(B, RAD), pl.ds(H, B), :] += ry[1]
    own = (pl.ds(RAD, B), pl.ds(H, B), slice(None))
    out[...] = u[own] * (p[own] * (1.0 / VIEWS))

    for c in (up_mate, down_mate, up_away, down_away, side_away, side_mate, diag_up, diag_down,
              pass_top, pass_bottom, mate_top, mate_bottom):
        c.wait_send()


def body(ny, nx, current, recorded, psf_depth, psf_rows, psf_cols):
    hbm = pl.BlockSpec(memory_space=pl.ANY)
    smem = pl.BlockSpec(memory_space=pltpu.SMEM)
    return pl.pallas_call(
        functools.partial(kernel, ny, nx),
        out_shape=jax.ShapeDtypeStruct((B, B, Z), F32),
        in_specs=[hbm, hbm, smem, smem, smem],
        out_specs=pl.BlockSpec(memory_space=pltpu.VMEM),
        scratch_shapes=[
            pltpu.VMEM((ROWS, COLS, Z), F32),
            pltpu.VMEM((ROWS, VIEWS * B, Z), F32),
            pltpu.VMEM((B, VIEWS * B, Z), F32),
            pltpu.VMEM((VIEWS, B, B, Z), F32),
            pltpu.VMEM((ROWS, COLS, Z), F32),
            pltpu.VMEM((2, RAD, B, Z), F32),
            pltpu.VMEM((B, H, Z), F32),
            pltpu.VMEM((B, H, Z), F32),
            pltpu.VMEM((2, RAD, H, Z), F32),
            pltpu.VMEM((2, RAD, H, Z), F32),
            pltpu.VMEM((3, VIEWS * B, 3 * COLS), BF16),
            pltpu.VMEM((3, COLS, 3 * Z), BF16),
            pltpu.VMEM((VIEWS, 3 * Z, Z), BF16),
            pltpu.VMEM((VIEWS, 3 * Z, Z), BF16),
            pltpu.SemaphoreType.DMA((2,)),
            pltpu.SemaphoreType.DMA((20,)),
            pltpu.SemaphoreType.DMA((20,)),
        ],
        compiler_params=pltpu.CompilerParams(
            collective_id=0, has_side_effects=True, vmem_limit_bytes=48 * 1024 * 1024),
        name="richardson_lucy",
    )(current, recorded, psf_depth, psf_rows, psf_cols)


def solution(mesh):
    placed = (P("gy", "gx", None), P(None, "gy", "gx", None), P(), P(), P())
    return jax.shard_map(
        functools.partial(body, mesh.shape["gy"], mesh.shape["gx"]),
        mesh=mesh, in_specs=placed, out_specs=P("gy", "gx", None), check_vma=False
    )
```

time: 629 us -> 62.6 us (0.10); the launches traced: 617 us -> 62.4 us
  other arithmetic: 251 us -> 0 us
  blocking collectives: 183 us -> 0 us
  waiting for transfers between devices: 81.4 us -> 0 us
  starting transfers between devices: 74.1 us -> 0 us
  Pallas kernels: 0 us -> 56.9 us
  local copies, waits for them, and re-layouts: 26.5 us -> 5.47 us
    add x11 -> x0, other arithmetic: 228 us -> none  [taps_valid(): result = term if result is None else result + term]
    all_to_all x8 -> x0, blocking collectives: 183 us -> none  [the longest x6 134 us: column_pass(): lax.all_to_all(volume[v], 'gx', split_axis=0, concat_axis=1, tiled=True)]
    ppermute x4 -> x0, waiting for transfers between devices: 81.4 us -> none  [the longest x2 46.4 us: with_halo(): lax.ppermute(head, axis, [((i + 1) % count, i) for i in range(ends)])]
    all_to_all x8 -> x0, starting transfers between devices: 60.2 us -> none  [the longest x6 50.3 us: column_pass(): lax.all_to_all(convolved, 'gx', split_axis=1, concat_axis=0, tiled=True)]
    pallas_call x0 -> x1, Pallas kernels: none -> 56.9 us  [body(): pl.pallas_call(functools.partial(kernel, ny, nx), out_shape=jax.ShapeDtyp...]
    reduce_sum x4 -> x0, other arithmetic: 17.8 us -> none  [the longest x1 16.7 us: body(): updated = current * (jnp.sum(backed, axis=0) / count)]
    mul x2 -> x0, local copies, waits for them, and re-layouts: 16 us -> none  [taps_valid(): term = weights[:, k].reshape((-1,) + (1,) * (padded.ndim - 1)) * window_part]
    ppermute x4 -> x0, starting transfers between devices: 13.9 us -> none  [the longest x2 10.8 us: with_halo(): lax.ppermute(tail, axis, [(i, (i + 1) % count) for i in range(ends)])]
  transfers between devices with their start and end apart: 12 -> 0, of which waited for: 4 -> 0; matrix products, arithmetic and copies ran while one was open for 32% -> 0% of each run, Pallas kernels for 0% -> 0%
where the time goes in v1:
time: 62.6 us; the launch traced here: 62.4 us
  Pallas kernels  56.9 us (91%)
  local copies, waits for them, and re-layouts  5.47 us (9%)
    pallas_call x1, Pallas kernels, body(): pl.pallas_call(functools.partial(kernel, ny, nx), out_shape=jax.ShapeDtyp...  56.9 us
    unnamed x11, local copies, waits for them, and re-layouts  5.47 us

profile of v1, /device:TPU:1, one launch (start us, length us, event | category | flops | bytes accessed | tf_op | source)
XLA Modules:
  0.0 62.4 jit_solution(11302663579683176908)
XLA Ops:
  0.0 0.0 copy-start
  0.0 1.6 %copy-done = f32[4,32,32,128]{3,2,1,0:T(8,128)S(1)} copy-done((f32[4,32,32,128]{3,2,1,0:T(8,128)S(1)}, f32[4,32,32,128]{3,2,1,0:T(8,128)}, u32[]{:S(2)}) %copy-start) | copy-done | bytes 2097176
  1.6 0.0 copy-start.1
  1.6 1.0 %copy-done.1 = f32[32,32,128]{2,1,0:T(8,128)S(1)} copy-done((f32[32,32,128]{2,1,0:T(8,128)S(1)}, f32[32,32,128]{2,1,0:T(8,128)}, u32[]{:S(2)}) %copy-start.1) | copy-done | bytes 524312
  2.6 0.0 copy-start.2
  2.6 0.7 %copy-done.2 = f32[4,31]{1,0:T(4,128)S(1)} copy-done((f32[4,31]{1,0:T(4,128)S(1)}, f32[4,31]{1,0:T(4,128)}, u32[]{:S(2)}) %copy-start.2) | copy-done | bytes 520
  3.3 0.0 copy-start.3
  3.3 0.7 %copy-done.3 = f32[4,31]{1,0:T(4,128)S(1)} copy-done((f32[4,31]{1,0:T(4,128)S(1)}, f32[4,31]{1,0:T(4,128)}, u32[]{:S(2)}) %copy-start.3) | copy-done | bytes 520
  4.0 0.0 copy-start.4
  4.0 0.7 %copy-done.4 = f32[4,31]{1,0:T(4,128)S(1)} copy-done((f32[4,31]{1,0:T(4,128)S(1)}, f32[4,31]{1,0:T(4,128)}, u32[]{:S(2)}) %copy-start.4) | copy-done | bytes 520
  4.7 56.9 %richardson_lucy.1 = f32[32,32,128]{2,1,0:T(8,128)S(1)} custom-call(f32[32,32,128]{2,1,0:T(8,128)S(1)} %copy-done.1, f32[4,32,32,128]{3,2,1,0:T(8,128)S(1)} %copy-done, f32[4,31]{1,0:T(4,128)S(1)} %copy-done.2, f32[4,31]{1,0:T(4,128)S(1)} %copy-done.3, f32[4,31]{1,0:T(4,128)S(1)} %copy-done.4), custom_call_target="tpu_custom_call" | custom-call | tf_op jit(solution)/shard_map/richardson_lucy/pallas_call | solution.py:324
  61.6 0.8 %copy.7 = f32[32,32,128]{2,1,0:T(8,128)} copy(f32[32,32,128]{2,1,0:T(8,128)S(1)} %richardson_lucy.1) | data formatting | bytes 1048576
Async XLA Ops:
  0.0 1.6 %copy-start = (f32[4,32,32,128]{3,2,1,0:T(8,128)S(1)}, f32[4,32,32,128]{3,2,1,0:T(8,128)}, u32[]{:S(2)}) copy-start(f32[4,32,32,128]{3,2,1,0:T(8,128)} %rec.1) | copy-start | bytes 6291460
  1.6 1.0 %copy-start.1 = (f32[32,32,128]{2,1,0:T(8,128)S(1)}, f32[32,32,128]{2,1,0:T(8,128)}, u32[]{:S(2)}) copy-start(f32[32,32,128]{2,1,0:T(8,128)} %cur.1) | copy-start | bytes 1572868
  2.6 0.7 %copy-start.2 = (f32[4,31]{1,0:T(4,128)S(1)}, f32[4,31]{1,0:T(4,128)}, u32[]{:S(2)}) copy-start(f32[4,31]{1,0:T(4,128)} %kz.1) | copy-start | bytes 1492
  3.3 0.7 %copy-start.3 = (f32[4,31]{1,0:T(4,128)S(1)}, f32[4,31]{1,0:T(4,128)}, u32[]{:S(2)}) copy-start(f32[4,31]{1,0:T(4,128)} %ky.1) | copy-start | bytes 1492
  4.0 0.7 %copy-start.4 = (f32[4,31]{1,0:T(4,128)S(1)}, f32[4,31]{1,0:T(4,128)}, u32[]{:S(2)}) copy-start(f32[4,31]{1,0:T(4,128)} %kx.1) | copy-start | bytes 1492

commit v2 on v1

--- a/solution.py
+++ b/solution.py
@@ -45,7 +45,7 @@
     return total
 
 
-def kernel(ny, nx, cur, rec, kz, ky, kx, out, u, xb, yb, rv, p, ry, rxp, rxo, rd, rpc,
+def kernel(ny, nx, cur, rec, kz, ky, kx, out, u, xb, yb, gb, rv, p, ry, rxp, rxo, rd, rpc,
            tf, tb, wf, wb, local_sem, send_sem, recv_sem):
     i = lax.axis_index("gy")
     j = lax.axis_index("gx")
@@ -72,32 +72,6 @@
     peers = [(up, j), (down, j), (i, away), (i, mate), (up, away), (down, away)]
     for peer in peers:
         pl.semaphore_signal(barrier, inc=1, device_id=peer, device_id_type=pl.DeviceIdType.MESH)
-    pl.semaphore_wait(barrier, len(peers))
-
-    def remote(k, src, dst, peer):
-        return pltpu.make_async_remote_copy(
-            src_ref=src, dst_ref=dst, send_sem=send_sem.at[k], recv_sem=recv_sem.at[k],
-            device_id=peer, device_id_type=pl.DeviceIdType.MESH)
-
-    top = pl.ds(0, RAD)
-    bottom = pl.ds(RAD + B, RAD)
-    mid = pl.ds(RAD, B)
-    first = pl.ds(0, RAD)
-    last = pl.ds(B - RAD, RAD)
-
-    up_mate = remote(0, cur.at[first, col(own_mate), :], u.at[bottom, col(H + own_mate), :], (up, j))
-    down_mate = remote(1, cur.at[last, col(own_mate), :], u.at[top, col(H + own_mate), :], (down, j))
-    up_away = remote(2, cur.at[first, col(own_away), :], u.at[bottom, col(H + own_away), :], (up, j))
-    down_away = remote(3, cur.at[last, col(own_away), :], u.at[top, col(H + own_away), :], (down, j))
-    side_away = remote(4, cur.at[:, col(own_away), :], u.at[mid, col(48 - halo_away), :], (i, away))
-    side_mate = remote(5, cur.at[:, col(own_mate), :], u.at[mid, col(48 - halo_mate), :], (i, mate))
-    diag_up = remote(6, cur.at[first, col(own_away), :], u.at[bottom, col(48 - halo_away), :], (up, away))
-    diag_down = remote(7, cur.at[last, col(own_away), :], u.at[top, col(48 - halo_away), :], (down, away))
-    pass_top = remote(8, u.at[top, col(H + own_mate), :], u.at[top, col(48 - halo_mate), :], (i, mate))
-    pass_bottom = remote(9, u.at[bottom, col(H + own_mate), :], u.at[bottom, col(48 - halo_mate), :], (i, mate))
-    for c in (side_mate, side_away, up_mate, down_mate, up_away, down_away, diag_up, diag_down):
-        c.start()
-
     row_id = lax.broadcasted_iota(jnp.int32, (B, Z), 0)
     lane_id = lax.broadcasted_iota(jnp.int32, (B, Z), 1)
     low = jnp.where(j == 0, H, 0)
@@ -142,6 +116,32 @@
 
     lax.fori_loop(0, VIEWS, depth_matrix, 0)
 
+    pl.semaphore_wait(barrier, len(peers))
+
+    def remote(k, src, dst, peer):
+        return pltpu.make_async_remote_copy(
+            src_ref=src, dst_ref=dst, send_sem=send_sem.at[k], recv_sem=recv_sem.at[k],
+            device_id=peer, device_id_type=pl.DeviceIdType.MESH)
+
+    top = pl.ds(0, RAD)
+    bottom = pl.ds(RAD + B, RAD)
+    mid = pl.ds(RAD, B)
+    first = pl.ds(0, RAD)
+    last = pl.ds(B - RAD, RAD)
+
+    up_mate = remote(0, cur.at[first, col(own_mate), :], u.at[bottom, col(H + own_mate), :], (up, j))
+    down_mate = remote(1, cur.at[last, col(own_mate), :], u.at[top, col(H + own_mate), :], (down, j))
+    up_away = remote(2, cur.at[first, col(own_away), :], u.at[bottom, col(H + own_away), :], (up, j))
+    down_away = remote(3, cur.at[last, col(own_away), :], u.at[top, col(H + own_away), :], (down, j))
+    side_away = remote(4, cur.at[:, col(own_away), :], u.at[mid, col(48 - halo_away), :], (i, away))
+    side_mate = remote(5, cur.at[:, col(own_mate), :], u.at[mid, col(48 - halo_mate), :], (i, mate))
+    diag_up = remote(6, cur.at[first, col(own_away), :], u.at[bottom, col(48 - halo_away), :], (up, away))
+    diag_down = remote(7, cur.at[last, col(own_away), :], u.at[top, col(48 - halo_away), :], (down, away))
+    pass_top = remote(8, u.at[top, col(H + own_mate), :], u.at[top, col(48 - halo_mate), :], (i, mate))
+    pass_bottom = remote(9, u.at[bottom, col(H + own_mate), :], u.at[bottom, col(48 - halo_mate), :], (i, mate))
+    for c in (side_mate, side_away, up_mate, down_mate, up_away, down_away, diag_up, diag_down):
+        c.start()
+
     def x_forward(start, count, n):
         data = jnp.concatenate([triple_rows(u[start + r]) for r in range(count)], axis=1)
         res = dot(tf[n], data)
@@ -220,15 +220,17 @@
     load_rec.wait()
 
     def depth(n, c):
-        v = n // 4
-        rows = pl.ds(pl.multiple_of(lax.rem(n, 4) * 8, 8), 8)
-        lines = pl.ds(pl.multiple_of(v * B, B), B)
-        blurred = dot(triple_lanes(yb[rows, lines, :].reshape(8 * B, Z)), wf[v])
-        quotient = rv[v, rows].reshape(8 * B, Z) / blurred
-        yb[rows, lines, :] = dot(triple_lanes(quotient), wb[v]).reshape(8, B, Z)
-        return c
-
-    lax.fori_loop(0, 16, depth, 0)
+        rows = pl.ds(pl.multiple_of(n * 8, 8), 8)
+        lines = [pl.ds(v * B, B) for v in range(VIEWS)]
+        data = [triple_lanes(yb[rows, lines[v], :].reshape(8 * B, Z)) for v in range(VIEWS)]
+        blurred = [dot(data[v], wf[v]) for v in range(VIEWS)]
+        data = [triple_lanes(rv[v, rows].reshape(8 * B, Z) / blurred[v]) for v in range(VIEWS)]
+        res = [dot(data[v], wb[v]) for v in range(VIEWS)]
+        for v in range(VIEWS):
+            gb[rows, lines[v], :] = res[v].reshape(8, B, Z)
+        return c
+
+    lax.fori_loop(0, 4, depth, 0)
 
     def y_backward(rows):
         def step(n, c):
@@ -238,7 +240,7 @@
             for group in rows:
                 acc = {}
                 for q in range(max(0, group[0] - TAPS + 1), min(B - 1, group[-1]) + 1):
-                    x = yb[q, off, :]
+                    x = gb[q, off, :]
                     for r in group:
                         if 0 <= r - q < TAPS:
                             term = w[r - q] * x
@@ -330,6 +332,7 @@
             pltpu.VMEM((ROWS, COLS, Z), F32),
             pltpu.VMEM((ROWS, VIEWS * B, Z), F32),
             pltpu.VMEM((B, VIEWS * B, Z), F32),
+            pltpu.VMEM((B, VIEWS * B, Z), F32),
             pltpu.VMEM((VIEWS, B, B, Z), F32),
             pltpu.VMEM((ROWS, COLS, Z), F32),
             pltpu.VMEM((2, RAD, B, Z), F32),
@@ -346,7 +349,7 @@
             pltpu.SemaphoreType.DMA((20,)),
         ],
         compiler_params=pltpu.CompilerParams(
-            collective_id=0, has_side_effects=True, vmem_limit_bytes=48 * 1024 * 1024),
+            collective_id=0, has_side_effects=True, vmem_limit_bytes=60 * 1024 * 1024),
         name="richardson_lucy",
     )(current, recorded, psf_depth, psf_rows, psf_cols)
 

time: 62.6 us -> 56.6 us (0.904)
  local copies, waits for them, and re-layouts: 5.47 us -> 1.87 us
  Pallas kernels: 56.9 us -> 54.6 us
    unnamed x11 -> x1, local copies, waits for them, and re-layouts: 5.47 us -> 1.87 us
    pallas_call x1, Pallas kernels: 56.9 us -> 54.6 us  [body(): pl.pallas_call(functools.partial(kernel, ny, nx), out_shape=jax.ShapeDtyp...]
where the time goes in v2:
time: 56.6 us; the launch traced here: 56.5 us
  Pallas kernels  54.6 us (96%)
  local copies, waits for them, and re-layouts  1.87 us (3%)
    pallas_call x1, Pallas kernels, body(): pl.pallas_call(functools.partial(kernel, ny, nx), out_shape=jax.ShapeDtyp...  54.6 us
    unnamed x1, local copies, waits for them, and re-layouts  1.87 us

profile of v2, /device:TPU:1, one launch (start us, length us, event | category | flops | bytes accessed | tf_op | source)
XLA Modules:
  0.0 56.5 jit_solution(18053212068681810860)
XLA Ops:
  0.0 54.6 %richardson_lucy.1 = f32[32,32,128]{2,1,0:T(8,128)} custom-call(f32[32,32,128]{2,1,0:T(8,128)} %cur.1, f32[4,32,32,128]{3,2,1,0:T(8,128)} %rec.1, f32[4,31]{1,0:T(4,128)} %kz.1, f32[4,31]{1,0:T(4,128)} %ky.1, f32[4,31]{1,0:T(4,128)} %kx.1), custom_call_target="tpu_custom_call" | custom-call | tf_op jit(solution)/shard_map/richardson_lucy/pallas_call | solution.py:326
  54.6 1.9 %copy.7 = f32[32,32,128]{2,1,0:T(8,128)} copy(f32[32,32,128]{2,1,0:T(8,128)} %richardson_lucy.1) | data formatting | bytes 1048576

commit v3 on v2

v3 whole, which is shorter than its diff:
```python
import functools

import jax
import jax.numpy as jnp
from jax import lax
from jax.experimental import pallas as pl
from jax.experimental.pallas import tpu as pltpu
from jax.sharding import PartitionSpec as P

F32 = jnp.float32
BF16 = jnp.bfloat16
TAPS = 31
RAD = 15
VIEWS = 4
B = 32
H = 16
ROWS = B + 2 * RAD
COLS = B + 2 * H
Z = 128


def split(x):
    hi = x.astype(BF16)
    return hi, (x - hi.astype(F32)).astype(BF16)


def triple_rows(x):
    hi, lo = split(x)
    return jnp.concatenate([hi, lo, hi], axis=0)


def triple_lanes(x):
    hi, lo = split(x)
    return jnp.concatenate([hi, lo, hi], axis=1)


def dot(a, b):
    return jnp.dot(a, b, preferred_element_type=F32)


def tap_sum(ref, v):
    total = ref[v, 0]
    for t in range(1, TAPS):
        total = total + ref[v, t]
    return total


def kernel(ny, nx, cur, rec, kz, ky, kx, out, u, xb, yb, gb, rv, p, ry, rxp, rxo, rup, rdn, rq, rpc,
           tf, tb, wf, wb, local_sem, send_sem, recv_sem):
    i = lax.axis_index("gy")
    j = lax.axis_index("gx")
    side = lax.rem(j, 2)
    up = lax.rem(i + ny - 1, ny)
    down = lax.rem(i + 1, ny)
    away = lax.rem(j + nx - 1 + 2 * side, nx)
    mate = j + 1 - 2 * side

    def col(x):
        return pl.ds(pl.multiple_of(x, H), H)

    own_away = H * side
    own_mate = H * (1 - side)
    halo_away = 48 * side
    halo_mate = 48 * (1 - side)

    load_rec = pltpu.make_async_copy(rec, rv, local_sem.at[0])
    load_cur = pltpu.make_async_copy(cur, u.at[pl.ds(RAD, B), pl.ds(H, B), :], local_sem.at[1])
    load_cur.start()
    load_rec.start()

    barrier = pltpu.get_barrier_semaphore()
    peers = [(up, j), (down, j), (i, away), (i, mate), (up, away), (down, away)]
    for peer in peers:
        pl.semaphore_signal(barrier, inc=1, device_id=peer, device_id_type=pl.DeviceIdType.MESH)
    pl.semaphore_wait(barrier, len(peers))

    count = [0]

    def remote(src, dst, peer):
        k = count[0]
        count[0] += 1
        return pltpu.make_async_remote_copy(
            src_ref=src, dst_ref=dst, send_sem=send_sem.at[k], recv_sem=recv_sem.at[k],
            device_id=peer, device_id_type=pl.DeviceIdType.MESH)

    near_top, far_top = pl.ds(7, 8), pl.ds(0, 7)
    near_bottom, far_bottom = pl.ds(47, 8), pl.ds(55, 7)
    top, bottom, mid = pl.ds(0, RAD), pl.ds(RAD + B, RAD), pl.ds(RAD, B)
    to_top = ((pl.ds(24, 8), near_top), (pl.ds(17, 7), far_top))
    to_bottom = ((pl.ds(0, 8), near_bottom), (pl.ds(8, 7), far_bottom))
    mine = H + own_away
    theirs = 48 - mine
    side_mate = remote(cur.at[:, col(own_mate), :], u.at[mid, col(48 - halo_mate), :], (i, mate))

    def corner(rows, peer):
        return [remote(cur.at[a, col(own_away), :], u.at[b, col(48 - halo_away), :], (peer, away)) for a, b in rows]

    def edge(rows, peer):
        return [remote(cur.at[a, col(own_mate), :], u.at[b, col(H + own_mate), :], (peer, j)) for a, b in rows]

    corner_up, corner_down = corner(to_bottom, up), corner(to_top, down)
    edge_up, edge_down = edge(to_bottom, up), edge(to_top, down)
    side_away = [remote(cur.at[pl.ds(r, n), col(own_away), :], u.at[pl.ds(RAD + r, n), col(48 - halo_away), :], (i, away))
                 for r, n in ((24, 8), (17, 7), (0, 17))]
    relay_down = [remote(u.at[pl.ds(RAD + r, n), col(halo_away), :], u.at[b, col(theirs), :], (down, away))
                  for r, n, b in ((24, 8, near_top), (17, 7, far_top))]
    relay_away = [remote(u.at[b, col(halo_away), :], u.at[b, col(theirs), :], (i, away))
                  for b in (near_bottom, far_bottom)]
    pass_top = [remote(u.at[b, col(H + own_mate), :], u.at[b, col(48 - halo_mate), :], (i, mate))
                for b in (near_top, far_top)]
    pass_bottom = [remote(u.at[b, col(H + own_mate), :], u.at[b, col(48 - halo_mate), :], (i, mate))
                   for b in (near_bottom, far_bottom)]
    for c in (side_mate, corner_up[0], side_away[0], corner_up[1], side_away[1], side_away[2],
              edge_down[0], edge_up[0], corner_down[0], edge_down[1], edge_up[1], corner_down[1]):
        c.start()

    row_id = lax.broadcasted_iota(jnp.int32, (B, Z), 0)
    lane_id = lax.broadcasted_iota(jnp.int32, (B, Z), 1)
    low = jnp.where(j == 0, H, 0)
    high = jnp.where(j == nx - 1, H + B, COLS)
    inside = (lane_id >= low) & (lane_id < high)
    parts = []
    for v in range(VIEWS):
        band = jnp.zeros((B, Z), F32)
        for t in range(TAPS):
            band = jnp.where(lane_id - row_id == t + 1, kx[v, t], band)
        band = band / jnp.full((B, Z), tap_sum(kx, v), F32)
        parts.append(jnp.where(inside, band, 0.0))
    full = jnp.concatenate(parts, axis=0)
    flipped = full.T[:COLS]
    keep_top = jnp.where(i == 0, 0.0, 1.0).astype(F32)
    keep_bottom = jnp.where(i == ny - 1, 0.0, 1.0).astype(F32)
    for n, keep in enumerate((None, keep_top, keep_bottom)):
        a = full if keep is None else full * keep
        b = flipped if keep is None else flipped * keep
        hi, lo = split(a[:, :COLS])
        tf[n, :, 0:COLS] = hi
        tf[n, :, COLS:2 * COLS] = hi
        tf[n, :, 2 * COLS:3 * COLS] = lo
        hi, lo = split(b)
        tb[n, :, 0:Z] = hi
        tb[n, :, Z:2 * Z] = hi
        tb[n, :, 2 * Z:3 * Z] = lo

    def depth_matrix(v, c):
        r = lax.broadcasted_iota(jnp.int32, (Z, Z), 0)
        l = lax.broadcasted_iota(jnp.int32, (Z, Z), 1)
        band = jnp.zeros((Z, Z), F32)
        for t in range(TAPS):
            band = jnp.where(r - l == t - RAD, kz[v, t], band)
        band = band / jnp.full((Z, Z), tap_sum(kz, v) * tap_sum(ky, v), F32)
        for ref, m in ((wf, band), (wb, band.T)):
            hi, lo = split(m)
            ref[v, 0:Z, :] = hi
            ref[v, Z:2 * Z, :] = hi
            ref[v, 2 * Z:3 * Z, :] = lo
        return c

    lax.fori_loop(0, VIEWS, depth_matrix, 0)

    def x_forward(start, count, n):
        data = jnp.concatenate([triple_rows(u[start + r]) for r in range(count)], axis=1)
        res = dot(tf[n], data)
        for r in range(count):
            xb[start + r] = res[:, r * Z:(r + 1) * Z]

    for n in range(2):
        corner_up[n].wait_recv()
        relay_away[n].start()
        side_away[n].wait_recv()
        relay_down[n].start()
    load_cur.wait()
    side_mate.wait_recv()
    side_away[2].wait_recv()

    def own_rows(g, c):
        x_forward(RAD + 4 * g, 4, 0)
        return c

    lax.fori_loop(0, B // 4, own_rows, 0)

    edge_down[0].wait_recv()
    pass_top[0].start()
    edge_up[0].wait_recv()
    pass_bottom[0].start()

    def y_forward_own(n, c):
        off = pl.ds(pl.multiple_of(n * 8, 8), 8)
        v = n // 4
        w = [ky[v, t] for t in range(TAPS)]
        for b in range(4):
            acc = [None] * 8
            for r in range(max(RAD, 8 * b), min(RAD + B - 1, 8 * b + 37) + 1):
                x = xb[r, off, :]
                for o in range(8):
                    t = r - (8 * b + o)
                    if 0 <= t < TAPS:
                        term = w[t] * x
                        acc[o] = term if acc[o] is None else acc[o] + term
            for o in range(8):
                yb[8 * b + o, off, :] = acc[o]
        return c

    lax.fori_loop(0, 16, y_forward_own, 0)

    edge_down[1].wait_recv()
    pass_top[1].start()
    edge_up[1].wait_recv()
    pass_bottom[1].start()

    def arrived(n):
        for c in (corner_down[n], relay_away[n], relay_down[n], pass_top[n], pass_bottom[n]):
            c.wait_recv()

    def y_forward_halo(rows):
        def step(n, c):
            off = pl.ds(pl.multiple_of(n * 8, 8), 8)
            v = n // 4
            w = [ky[v, t] for t in range(TAPS)]
            for b in range(4):
                outs = [8 * b + o for o in range(8)]
                acc = {}
                for r in rows:
                    hits = [o for o in outs if 0 <= r - o < TAPS]
                    if not hits:
                        continue
                    x = xb[r, off, :]
                    for o in hits:
                        term = w[r - o] * x
                        acc[o] = acc[o] + term if o in acc else term
                for o, a in acc.items():
                    yb[o, off, :] += a
            return c

        lax.fori_loop(0, 16, step, 0)

    def depth(n, c):
        rows = pl.ds(pl.multiple_of(n * 8, 8), 8)
        lines = [pl.ds(v * B, B) for v in range(VIEWS)]
        data = [triple_lanes(yb[rows, lines[v], :].reshape(8 * B, Z)) for v in range(VIEWS)]
        blurred = [dot(data[v], wf[v]) for v in range(VIEWS)]
        data = [triple_lanes(rv[v, rows].reshape(8 * B, Z) / blurred[v]) for v in range(VIEWS)]
        res = [dot(data[v], wb[v]) for v in range(VIEWS)]
        for v in range(VIEWS):
            gb[rows, lines[v], :] = res[v].reshape(8, B, Z)
        return c

    def near_rows(g, c):
        x_forward(7 + 4 * g, 4, 1)
        x_forward(47 + 4 * g, 4, 2)
        return c

    def far_rows(g, c):
        x_forward(3 * g, 4, 1)
        x_forward(55 + 3 * g, 4, 2)
        return c

    arrived(0)
    lax.fori_loop(0, 2, near_rows, 0)
    y_forward_halo(list(range(7, 15)) + list(range(47, 55)))
    load_rec.wait()
    lax.fori_loop(1, 3, depth, 0)
    arrived(1)
    lax.fori_loop(0, 2, far_rows, 0)
    y_forward_halo(list(range(0, 7)) + list(range(55, 62)))
    lax.fori_loop(0, 2, lambda n, c: depth(3 * n, c), 0)

    def y_backward(rows):
        def step(n, c):
            off = pl.ds(pl.multiple_of(n * 8, 8), 8)
            v = n // 4
            w = [ky[v, t] for t in range(TAPS)]
            for group in rows:
                acc = {}
                for q in range(max(0, group[0] - TAPS + 1), min(B - 1, group[-1]) + 1):
                    x = gb[q, off, :]
                    for r in group:
                        if 0 <= r - q < TAPS:
                            term = w[r - q] * x
                            acc[r] = acc[r] + term if r in acc else term
                for r, a in acc.items():
                    xb[r, off, :] = a
            return c

        lax.fori_loop(0, 16, step, 0)

    def x_backward(start, count, n):
        data = jnp.concatenate([triple_rows(xb[start + r]) for r in range(count)], axis=1)
        res = dot(tb[n], data)
        for r in range(count):
            p[start + r] = res[:, r * Z:(r + 1) * Z]

    wide = pl.ds(pl.multiple_of(32 * side, 32), B)
    mate_bottom = remote(p.at[bottom, col(halo_mate), :], rpc.at[1], (i, mate))
    mate_top = remote(p.at[top, col(halo_mate), :], rpc.at[0], (i, mate))
    sum_away = remote(p.at[bottom, col(mine), :], rq, (i, away))
    sum_up = remote(p.at[top, wide, :], rup, (up, away))
    sum_down = remote(p.at[bottom, col(halo_away), :], rdn, (down, away))
    back_up = remote(p.at[top, col(H + own_mate), :], ry.at[1], (up, j))
    back_down = remote(p.at[bottom, col(H + own_mate), :], ry.at[0], (down, j))
    back_mate = remote(p.at[mid, col(halo_mate), :], rxp, (i, mate))
    upper, lower = pl.ds(RAD, B - RAD), pl.ds(B, RAD)
    back_away = [remote(p.at[a, col(halo_away), :], rxo.at[b], (i, away))
                 for a, b in ((upper, pl.ds(0, B - RAD)), (lower, pl.ds(B - RAD, RAD)))]

    def halo_back(start, n):
        def step(g, c):
            x_backward(start + jnp.minimum(4 * g, RAD - 4), 4, n)
            return c

        lax.fori_loop(0, 4, step, 0)

    y_backward([range(47, 55), range(55, 62)])
    halo_back(RAD + B, 2)
    sum_away.start()
    mate_bottom.start()
    y_backward([range(0, 8), range(8, 15)])
    halo_back(0, 1)
    sum_up.start()
    mate_top.start()
    mate_bottom.wait_recv()
    p[bottom, col(H + own_mate), :] += rpc[1]
    back_down.start()
    mate_top.wait_recv()
    p[top, col(H + own_mate), :] += rpc[0]
    back_up.start()

    y_backward([range(RAD + 8 * b, RAD + 8 * b + 8) for b in range(4)])
    sum_away.wait_recv()
    p[bottom, col(halo_away), :] += rq[...]
    sum_down.start()

    def own_back(g, c):
        x_backward(RAD + 4 * g, 4, 0)
        return c

    lax.fori_loop(0, B // 4, own_back, 0)
    back_away[0].start()
    back_mate.start()
    sum_up.wait_recv()
    p[lower, wide, :] += rup[...]
    back_away[1].start()

    back_mate.wait_recv()
    p[mid, col(H + own_mate), :] += rxp[...]
    back_down.wait_recv()
    p[pl.ds(RAD, RAD), col(H + own_mate), :] += ry[0]
    back_up.wait_recv()
    p[lower, col(H + own_mate), :] += ry[1]
    sum_down.wait_recv()
    p[pl.ds(RAD, RAD), col(mine), :] += rdn[...]
    back_away[0].wait_recv()
    back_away[1].wait_recv()
    p[mid, col(mine), :] += rxo[...]
    own = (mid, pl.ds(H, B), slice(None))
    out[...] = u[own] * (p[own] * (1.0 / VIEWS))

    for c in (side_mate, *corner_up, *corner_down, *edge_up, *edge_down, *side_away, *relay_down, *relay_away,
              *pass_top, *pass_bottom, mate_bottom, mate_top, sum_away, sum_up, sum_down, back_up, back_down,
              back_mate, *back_away):
        c.wait_send()


def body(ny, nx, current, recorded, psf_depth, psf_rows, psf_cols):
    hbm = pl.BlockSpec(memory_space=pl.ANY)
    smem = pl.BlockSpec(memory_space=pltpu.SMEM)
    return pl.pallas_call(
        functools.partial(kernel, ny, nx),
        out_shape=jax.ShapeDtypeStruct((B, B, Z), F32),
        in_specs=[hbm, hbm, smem, smem, smem],
        out_specs=pl.BlockSpec(memory_space=pltpu.VMEM),
        scratch_shapes=[
            pltpu.VMEM((ROWS, COLS, Z), F32),
            pltpu.VMEM((ROWS, VIEWS * B, Z), F32),
            pltpu.VMEM((B, VIEWS * B, Z), F32),
            pltpu.VMEM((B, VIEWS * B, Z), F32),
            pltpu.VMEM((VIEWS, B, B, Z), F32),
            pltpu.VMEM((ROWS, COLS, Z), F32),
            pltpu.VMEM((2, RAD, H, Z), F32),
            pltpu.VMEM((B, H, Z), F32),
            pltpu.VMEM((B, H, Z), F32),
            pltpu.VMEM((RAD, B, Z), F32),
            pltpu.VMEM((RAD, H, Z), F32),
            pltpu.VMEM((RAD, H, Z), F32),
            pltpu.VMEM((2, RAD, H, Z), F32),
            pltpu.VMEM((3, VIEWS * B, 3 * COLS), BF16),
            pltpu.VMEM((3, COLS, 3 * Z), BF16),
            pltpu.VMEM((VIEWS, 3 * Z, Z), BF16),
            pltpu.VMEM((VIEWS, 3 * Z, Z), BF16),
            pltpu.SemaphoreType.DMA((2,)),
            pltpu.SemaphoreType.DMA((32,)),
            pltpu.SemaphoreType.DMA((32,)),
        ],
        compiler_params=pltpu.CompilerParams(
            collective_id=0, has_side_effects=True, vmem_limit_bytes=60 * 1024 * 1024),
        name="richardson_lucy",
    )(current, recorded, psf_depth, psf_rows, psf_cols)


def solution(mesh):
    placed = (P("gy", "gx", None), P(None, "gy", "gx", None), P(), P(), P())
    return jax.shard_map(
        functools.partial(body, mesh.shape["gy"], mesh.shape["gx"]),
        mesh=mesh, in_specs=placed, out_specs=P("gy", "gx", None), check_vma=False
    )
```

time: 56.6 us -> 54 us (0.954)
  Pallas kernels: 54.6 us -> 52 us
    pallas_call x1, Pallas kernels: 54.6 us -> 52 us  [body(): pl.pallas_call(functools.partial(kernel, ny, nx), out_shape=jax.ShapeDtyp...]
where the time goes in v3:
time: 54 us; the launch traced here: 53.8 us
  Pallas kernels  52 us (96%)
  local copies, waits for them, and re-layouts  1.87 us (3%)
    pallas_call x1, Pallas kernels, body(): pl.pallas_call(functools.partial(kernel, ny, nx), out_shape=jax.ShapeDtyp...  52 us
    unnamed x1, local copies, waits for them, and re-layouts  1.87 us

profile of v3, /device:TPU:1, one launch (start us, length us, event | category | flops | bytes accessed | tf_op | source)
XLA Modules:
  0.0 53.8 jit_solution(15208307726858565208)
XLA Ops:
  0.0 52.0 %richardson_lucy.1 = f32[32,32,128]{2,1,0:T(8,128)} custom-call(f32[32,32,128]{2,1,0:T(8,128)} %cur.1, f32[4,32,32,128]{3,2,1,0:T(8,128)} %rec.1, f32[4,31]{1,0:T(4,128)} %kz.1, f32[4,31]{1,0:T(4,128)} %ky.1, f32[4,31]{1,0:T(4,128)} %kx.1), custom_call_target="tpu_custom_call" | custom-call | tf_op jit(solution)/shard_map/richardson_lucy/pallas_call | solution.py:367
  52.0 1.9 %copy.7 = f32[32,32,128]{2,1,0:T(8,128)} copy(f32[32,32,128]{2,1,0:T(8,128)} %richardson_lucy.1) | data formatting | bytes 1048576

commit v4 on v3

--- a/solution.py
+++ b/solution.py
@@ -14,6 +14,7 @@
 VIEWS = 4
 B = 32
 H = 16
+HL = 64
 ROWS = B + 2 * RAD
 COLS = B + 2 * H
 Z = 128
@@ -46,7 +47,7 @@
 
 
 def kernel(ny, nx, cur, rec, kz, ky, kx, out, u, xb, yb, gb, rv, p, ry, rxp, rxo, rup, rdn, rq, rpc,
-           tf, tb, wf, wb, local_sem, send_sem, recv_sem):
+           tf, tfm, tb, wf, wb, local_sem, send_sem, recv_sem):
     i = lax.axis_index("gy")
     j = lax.axis_index("gx")
     side = lax.rem(j, 2)
@@ -110,23 +111,35 @@
                 for b in (near_top, far_top)]
     pass_bottom = [remote(u.at[b, col(H + own_mate), :], u.at[b, col(48 - halo_mate), :], (i, mate))
                    for b in (near_bottom, far_bottom)]
-    for c in (side_mate, corner_up[0], side_away[0], corner_up[1], side_away[1], side_away[2],
-              edge_down[0], edge_up[0], corner_down[0], edge_down[1], edge_up[1], corner_down[1]):
-        c.start()
-
-    row_id = lax.broadcasted_iota(jnp.int32, (B, Z), 0)
-    lane_id = lax.broadcasted_iota(jnp.int32, (B, Z), 1)
+    side_mate.start()
+    corner_up[0].start()
+    side_away[0].start()
+    corner_up[1].start()
+    side_away[1].start()
+    side_away[2].start()
+    edge_down[0].start()
+    edge_up[0].start()
+    corner_down[0].start()
+
+    row_id = lax.broadcasted_iota(jnp.int32, (H, Z), 0)
+    lane_id = lax.broadcasted_iota(jnp.int32, (H, Z), 1)
     low = jnp.where(j == 0, H, 0)
     high = jnp.where(j == nx - 1, H + B, COLS)
-    inside = (lane_id >= low) & (lane_id < high)
-    parts = []
-    for v in range(VIEWS):
-        band = jnp.zeros((B, Z), F32)
-        for t in range(TAPS):
-            band = jnp.where(lane_id - row_id == t + 1, kx[v, t], band)
-        band = band / jnp.full((B, Z), tap_sum(kx, v), F32)
-        parts.append(jnp.where(inside, band, 0.0))
-    full = jnp.concatenate(parts, axis=0)
+    def column_bands(half, base):
+        parts = []
+        for v in range(VIEWS):
+            band = jnp.zeros((H, Z), F32)
+            for t in range(TAPS):
+                band = jnp.where(lane_id - row_id == half - base + t + 1, kx[v, t], band)
+            band = band / jnp.full((H, Z), tap_sum(kx, v), F32)
+            parts.append(jnp.where((lane_id >= low - base) & (lane_id < high - base), band, 0.0))
+        return jnp.concatenate(parts, axis=0)
+
+    full = jnp.concatenate([column_bands(own_mate, 0), column_bands(own_away, 0)], axis=0)
+    hi, lo = split(column_bands(own_mate, own_mate)[:, :COLS])
+    tfm[:, 0:COLS] = hi
+    tfm[:, COLS:2 * COLS] = hi
+    tfm[:, 2 * COLS:3 * COLS] = lo
     flipped = full.T[:COLS]
     keep_top = jnp.where(i == 0, 0.0, 1.0).astype(F32)
     keep_bottom = jnp.where(i == ny - 1, 0.0, 1.0).astype(F32)
@@ -158,35 +171,35 @@
 
     lax.fori_loop(0, VIEWS, depth_matrix, 0)
 
-    def x_forward(start, count, n):
+    def x_forward(start, count, n, lines=(0, 2 * HL)):
         data = jnp.concatenate([triple_rows(u[start + r]) for r in range(count)], axis=1)
-        res = dot(tf[n], data)
+        res = dot(tf[n, lines[0]:lines[1]], data)
         for r in range(count):
-            xb[start + r] = res[:, r * Z:(r + 1) * Z]
-
-    for n in range(2):
-        corner_up[n].wait_recv()
-        relay_away[n].start()
-        side_away[n].wait_recv()
-        relay_down[n].start()
-    load_cur.wait()
-    side_mate.wait_recv()
-    side_away[2].wait_recv()
-
-    def own_rows(g, c):
-        x_forward(RAD + 4 * g, 4, 0)
-        return c
-
-    lax.fori_loop(0, B // 4, own_rows, 0)
-
-    edge_down[0].wait_recv()
-    pass_top[0].start()
-    edge_up[0].wait_recv()
-    pass_bottom[0].start()
+            xb[start + r, lines[0]:lines[1]] = res[:, r * Z:(r + 1) * Z]
+
+    def mate_rows():
+        def step(g, c):
+            reach = pl.ds(pl.multiple_of(own_mate, H), 3 * H)
+            none = jnp.zeros((H, Z), F32)
+            data = jnp.concatenate(
+                [triple_rows(jnp.concatenate([u[RAD + 4 * g + r, reach, :], none], axis=0)) for r in range(4)], axis=1)
+            res = dot(tfm[...], data)
+            for r in range(4):
+                xb[RAD + 4 * g + r, 0:HL] = res[:, r * Z:(r + 1) * Z]
+            return c
+
+        lax.fori_loop(0, B // 4, step, 0)
+
+    def own_rows(lines):
+        def step(g, c):
+            x_forward(RAD + 4 * g, 4, 0, lines)
+            return c
+
+        lax.fori_loop(0, B // 4, step, 0)
 
     def y_forward_own(n, c):
         off = pl.ds(pl.multiple_of(n * 8, 8), 8)
-        v = n // 4
+        v = lax.rem(n // 2, VIEWS)
         w = [ky[v, t] for t in range(TAPS)]
         for b in range(4):
             acc = [None] * 8
@@ -201,8 +214,28 @@
                 yb[8 * b + o, off, :] = acc[o]
         return c
 
-    lax.fori_loop(0, 16, y_forward_own, 0)
-
+    load_cur.wait()
+    side_mate.wait_recv()
+    mate_rows()
+    lax.fori_loop(0, 8, y_forward_own, 0)
+    corner_up[0].wait_recv()
+    relay_away[0].start()
+    side_away[0].wait_recv()
+    relay_down[0].start()
+    corner_up[1].wait_recv()
+    side_away[1].wait_recv()
+    side_away[2].wait_recv()
+    edge_down[1].start()
+    edge_up[1].start()
+    corner_down[1].start()
+    relay_away[1].start()
+    relay_down[1].start()
+    own_rows((HL, 2 * HL))
+    lax.fori_loop(8, 16, y_forward_own, 0)
+    edge_down[0].wait_recv()
+    pass_top[0].start()
+    edge_up[0].wait_recv()
+    pass_bottom[0].start()
     edge_down[1].wait_recv()
     pass_top[1].start()
     edge_up[1].wait_recv()
@@ -215,7 +248,7 @@
     def y_forward_halo(rows):
         def step(n, c):
             off = pl.ds(pl.multiple_of(n * 8, 8), 8)
-            v = n // 4
+            v = lax.rem(n // 2, VIEWS)
             w = [ky[v, t] for t in range(TAPS)]
             for b in range(4):
                 outs = [8 * b + o for o in range(8)]
@@ -236,13 +269,20 @@
 
     def depth(n, c):
         rows = pl.ds(pl.multiple_of(n * 8, 8), 8)
-        lines = [pl.ds(v * B, B) for v in range(VIEWS)]
-        data = [triple_lanes(yb[rows, lines[v], :].reshape(8 * B, Z)) for v in range(VIEWS)]
+        lines = [[pl.ds(h * HL + v * H, H) for h in range(2)] for v in range(VIEWS)]
+        halves = (col(own_mate), col(own_away))
+
+        def flat(x, y):
+            return jnp.concatenate([x.reshape(8 * H, Z), y.reshape(8 * H, Z)], axis=0)
+
+        data = [triple_lanes(flat(*(yb[rows, q, :] for q in lines[v]))) for v in range(VIEWS)]
         blurred = [dot(data[v], wf[v]) for v in range(VIEWS)]
-        data = [triple_lanes(rv[v, rows].reshape(8 * B, Z) / blurred[v]) for v in range(VIEWS)]
+        images = [flat(*(rv[v, rows, q, :] for q in halves)) for v in range(VIEWS)]
+        data = [triple_lanes(images[v] / blurred[v]) for v in range(VIEWS)]
         res = [dot(data[v], wb[v]) for v in range(VIEWS)]
         for v in range(VIEWS):
-            gb[rows, lines[v], :] = res[v].reshape(8, B, Z)
+            for h in range(2):
+                gb[rows, lines[v][h], :] = res[v][h * 8 * H:(h + 1) * 8 * H].reshape(8, H, Z)
         return c
 
     def near_rows(g, c):
@@ -268,7 +308,7 @@
     def y_backward(rows):
         def step(n, c):
             off = pl.ds(pl.multiple_of(n * 8, 8), 8)
-            v = n // 4
+            v = lax.rem(n // 2, VIEWS)
             w = [ky[v, t] for t in range(TAPS)]
             for group in rows:
                 acc = {}
@@ -290,11 +330,11 @@
         for r in range(count):
             p[start + r] = res[:, r * Z:(r + 1) * Z]
 
-    wide = pl.ds(pl.multiple_of(32 * side, 32), B)
     mate_bottom = remote(p.at[bottom, col(halo_mate), :], rpc.at[1], (i, mate))
     mate_top = remote(p.at[top, col(halo_mate), :], rpc.at[0], (i, mate))
     sum_away = remote(p.at[bottom, col(mine), :], rq, (i, away))
-    sum_up = remote(p.at[top, wide, :], rup, (up, away))
+    sum_up = remote(p.at[top, col(mine), :], rup.at[0], (up, away))
+    sum_corner = remote(p.at[top, col(halo_away), :], rup.at[1], (up, away))
     sum_down = remote(p.at[bottom, col(halo_away), :], rdn, (down, away))
     back_up = remote(p.at[top, col(H + own_mate), :], ry.at[1], (up, j))
     back_down = remote(p.at[bottom, col(H + own_mate), :], ry.at[0], (down, j))
@@ -324,6 +364,7 @@
     mate_top.wait_recv()
     p[top, col(H + own_mate), :] += rpc[0]
     back_up.start()
+    sum_corner.start()
 
     y_backward([range(RAD + 8 * b, RAD + 8 * b + 8) for b in range(4)])
     sum_away.wait_recv()
@@ -338,7 +379,7 @@
     back_away[0].start()
     back_mate.start()
     sum_up.wait_recv()
-    p[lower, wide, :] += rup[...]
+    p[lower, col(halo_away), :] += rup[0]
     back_away[1].start()
 
     back_mate.wait_recv()
@@ -347,6 +388,8 @@
     p[pl.ds(RAD, RAD), col(H + own_mate), :] += ry[0]
     back_up.wait_recv()
     p[lower, col(H + own_mate), :] += ry[1]
+    sum_corner.wait_recv()
+    p[lower, col(mine), :] += rup[1]
     sum_down.wait_recv()
     p[pl.ds(RAD, RAD), col(mine), :] += rdn[...]
     back_away[0].wait_recv()
@@ -356,7 +399,7 @@
     out[...] = u[own] * (p[own] * (1.0 / VIEWS))
 
     for c in (side_mate, *corner_up, *corner_down, *edge_up, *edge_down, *side_away, *relay_down, *relay_away,
-              *pass_top, *pass_bottom, mate_bottom, mate_top, sum_away, sum_up, sum_down, back_up, back_down,
+              *pass_top, *pass_bottom, mate_bottom, mate_top, sum_away, sum_up, sum_corner, sum_down, back_up, back_down,
               back_mate, *back_away):
         c.wait_send()
 
@@ -379,11 +422,12 @@
             pltpu.VMEM((2, RAD, H, Z), F32),
             pltpu.VMEM((B, H, Z), F32),
             pltpu.VMEM((B, H, Z), F32),
-            pltpu.VMEM((RAD, B, Z), F32),
+            pltpu.VMEM((2, RAD, H, Z), F32),
             pltpu.VMEM((RAD, H, Z), F32),
             pltpu.VMEM((RAD, H, Z), F32),
             pltpu.VMEM((2, RAD, H, Z), F32),
             pltpu.VMEM((3, VIEWS * B, 3 * COLS), BF16),
+            pltpu.VMEM((HL, 3 * COLS), BF16),
             pltpu.VMEM((3, COLS, 3 * Z), BF16),
             pltpu.VMEM((VIEWS, 3 * Z, Z), BF16),
             pltpu.VMEM((VIEWS, 3 * Z, Z), BF16),

time: 54 us -> 52.9 us (0.980)
  Pallas kernels: 52 us -> 50.8 us
    pallas_call x1, Pallas kernels: 52 us -> 50.8 us  [body(): pl.pallas_call(functools.partial(kernel, ny, nx), out_shape=jax.ShapeDtyp...]
where the time goes in v4:
time: 52.9 us; the launch traced here: 52.7 us
  Pallas kernels  50.8 us (96%)
  local copies, waits for them, and re-layouts  1.87 us (4%)
    pallas_call x1, Pallas kernels, body(): pl.pallas_call(functools.partial(kernel, ny, nx), out_shape=jax.ShapeDtyp...  50.8 us
    unnamed x1, local copies, waits for them, and re-layouts  1.87 us

profile of v4, /device:TPU:1, one launch (start us, length us, event | category | flops | bytes accessed | tf_op | source)
XLA Modules:
  0.0 52.7 jit_solution(3558609538518630699)
XLA Ops:
  0.0 50.8 %richardson_lucy.1 = f32[32,32,128]{2,1,0:T(8,128)} custom-call(f32[32,32,128]{2,1,0:T(8,128)} %cur.1, f32[4,32,32,128]{3,2,1,0:T(8,128)} %rec.1, f32[4,31]{1,0:T(4,128)} %kz.1, f32[4,31]{1,0:T(4,128)} %ky.1, f32[4,31]{1,0:T(4,128)} %kx.1), custom_call_target="tpu_custom_call" | custom-call | tf_op jit(solution)/shard_map/richardson_lucy/pallas_call | solution.py:410
  50.8 1.9 %copy.7 = f32[32,32,128]{2,1,0:T(8,128)} copy(f32[32,32,128]{2,1,0:T(8,128)} %richardson_lucy.1) | data formatting | bytes 1048576

commit v5 on v4

--- a/solution.py
+++ b/solution.py
@@ -241,10 +241,6 @@
     edge_up[1].wait_recv()
     pass_bottom[1].start()
 
-    def arrived(n):
-        for c in (corner_down[n], relay_away[n], relay_down[n], pass_top[n], pass_bottom[n]):
-            c.wait_recv()
-
     def y_forward_halo(rows):
         def step(n, c):
             off = pl.ds(pl.multiple_of(n * 8, 8), 8)
@@ -265,7 +261,7 @@
                     yb[o, off, :] += a
             return c
 
-        lax.fori_loop(0, 16, step, 0)
+        lax.fori_loop(0, 16, step, 0, unroll=2)
 
     def depth(n, c):
         rows = pl.ds(pl.multiple_of(n * 8, 8), 8)
@@ -290,21 +286,16 @@
         x_forward(47 + 4 * g, 4, 2)
         return c
 
-    def far_rows(g, c):
-        x_forward(3 * g, 4, 1)
-        x_forward(55 + 3 * g, 4, 2)
-        return c
-
-    arrived(0)
-    lax.fori_loop(0, 2, near_rows, 0)
+    def far_rows(start, n):
+        x_forward(start, 4, n)
+        x_forward(start + 3, 4, n)
+
+    for c in (corner_down[0], relay_away[0], relay_down[0], pass_top[0], pass_bottom[0]):
+        c.wait_recv()
+    lax.fori_loop(0, 2, near_rows, 0, unroll=2)
     y_forward_halo(list(range(7, 15)) + list(range(47, 55)))
     load_rec.wait()
     lax.fori_loop(1, 3, depth, 0)
-    arrived(1)
-    lax.fori_loop(0, 2, far_rows, 0)
-    y_forward_halo(list(range(0, 7)) + list(range(55, 62)))
-    lax.fori_loop(0, 2, lambda n, c: depth(3 * n, c), 0)
-
     def y_backward(rows):
         def step(n, c):
             off = pl.ds(pl.multiple_of(n * 8, 8), 8)
@@ -322,7 +313,7 @@
                     xb[r, off, :] = a
             return c
 
-        lax.fori_loop(0, 16, step, 0)
+        lax.fori_loop(0, 16, step, 0, unroll=2)
 
     def x_backward(start, count, n):
         data = jnp.concatenate([triple_rows(xb[start + r]) for r in range(count)], axis=1)
@@ -348,28 +339,38 @@
             x_backward(start + jnp.minimum(4 * g, RAD - 4), 4, n)
             return c
 
-        lax.fori_loop(0, 4, step, 0)
-
+        lax.fori_loop(0, 4, step, 0, unroll=4)
+
+    relay_away[1].wait_recv()
+    pass_bottom[1].wait_recv()
+    far_rows(55, 2)
+    y_forward_halo(list(range(55, 62)))
+    depth(3, 0)
     y_backward([range(47, 55), range(55, 62)])
     halo_back(RAD + B, 2)
     sum_away.start()
     mate_bottom.start()
+    for c in (corner_down[1], relay_down[1], pass_top[1]):
+        c.wait_recv()
+    far_rows(0, 1)
+    y_forward_halo(list(range(0, 7)))
+    depth(0, 0)
+    mate_bottom.wait_recv()
+    p[bottom, col(H + own_mate), :] += rpc[1]
+    back_down.start()
     y_backward([range(0, 8), range(8, 15)])
     halo_back(0, 1)
     sum_up.start()
     mate_top.start()
-    mate_bottom.wait_recv()
-    p[bottom, col(H + own_mate), :] += rpc[1]
-    back_down.start()
+    sum_away.wait_recv()
+    p[bottom, col(halo_away), :] += rq[...]
+    sum_down.start()
     mate_top.wait_recv()
     p[top, col(H + own_mate), :] += rpc[0]
     back_up.start()
     sum_corner.start()
 
     y_backward([range(RAD + 8 * b, RAD + 8 * b + 8) for b in range(4)])
-    sum_away.wait_recv()
-    p[bottom, col(halo_away), :] += rq[...]
-    sum_down.start()
 
     def own_back(g, c):
         x_backward(RAD + 4 * g, 4, 0)

time: 52.9 us -> 50.3 us (0.951)
  Pallas kernels: 50.8 us -> 48.3 us
    pallas_call x1, Pallas kernels: 50.8 us -> 48.3 us  [body(): pl.pallas_call(functools.partial(kernel, ny, nx), out_shape=jax.ShapeDtyp...]
where the time goes in v5:
time: 50.3 us; the launch traced here: 50.2 us
  Pallas kernels  48.3 us (96%)
  local copies, waits for them, and re-layouts  1.87 us (4%)
    pallas_call x1, Pallas kernels, body(): pl.pallas_call(functools.partial(kernel, ny, nx), out_shape=jax.ShapeDtyp...  48.3 us
    unnamed x1, local copies, waits for them, and re-layouts  1.87 us

profile of v5, /device:TPU:1, one launch (start us, length us, event | category | flops | bytes accessed | tf_op | source)
XLA Modules:
  0.0 50.2 jit_solution(5370826535580941490)
XLA Ops:
  0.0 48.3 %richardson_lucy.1 = f32[32,32,128]{2,1,0:T(8,128)} custom-call(f32[32,32,128]{2,1,0:T(8,128)} %cur.1, f32[4,32,32,128]{3,2,1,0:T(8,128)} %rec.1, f32[4,31]{1,0:T(4,128)} %kz.1, f32[4,31]{1,0:T(4,128)} %ky.1, f32[4,31]{1,0:T(4,128)} %kx.1), custom_call_target="tpu_custom_call" | custom-call | tf_op jit(solution)/shard_map/richardson_lucy/pallas_call | solution.py:411
  48.3 1.9 %copy.7 = f32[32,32,128]{2,1,0:T(8,128)} copy(f32[32,32,128]{2,1,0:T(8,128)} %richardson_lucy.1) | data formatting | bytes 1048576

commit v6 on v5

--- a/solution.py
+++ b/solution.py
@@ -113,13 +113,12 @@
                    for b in (near_bottom, far_bottom)]
     side_mate.start()
     corner_up[0].start()
+    corner_up[1].start()
     side_away[0].start()
-    corner_up[1].start()
     side_away[1].start()
     side_away[2].start()
-    edge_down[0].start()
     edge_up[0].start()
-    corner_down[0].start()
+    edge_up[1].start()
 
     row_id = lax.broadcasted_iota(jnp.int32, (H, Z), 0)
     lane_id = lax.broadcasted_iota(jnp.int32, (H, Z), 1)
@@ -219,25 +218,22 @@
     mate_rows()
     lax.fori_loop(0, 8, y_forward_own, 0)
     corner_up[0].wait_recv()
+    corner_up[1].wait_recv()
     relay_away[0].start()
+    relay_away[1].start()
+    corner_down[0].start()
+    corner_down[1].start()
     side_away[0].wait_recv()
     relay_down[0].start()
-    corner_up[1].wait_recv()
     side_away[1].wait_recv()
+    relay_down[1].start()
     side_away[2].wait_recv()
+    edge_down[0].start()
     edge_down[1].start()
-    edge_up[1].start()
-    corner_down[1].start()
-    relay_away[1].start()
-    relay_down[1].start()
     own_rows((HL, 2 * HL))
     lax.fori_loop(8, 16, y_forward_own, 0)
-    edge_down[0].wait_recv()
-    pass_top[0].start()
     edge_up[0].wait_recv()
     pass_bottom[0].start()
-    edge_down[1].wait_recv()
-    pass_top[1].start()
     edge_up[1].wait_recv()
     pass_bottom[1].start()
 
@@ -281,21 +277,10 @@
                 gb[rows, lines[v][h], :] = res[v][h * 8 * H:(h + 1) * 8 * H].reshape(8, H, Z)
         return c
 
-    def near_rows(g, c):
-        x_forward(7 + 4 * g, 4, 1)
-        x_forward(47 + 4 * g, 4, 2)
-        return c
-
-    def far_rows(start, n):
-        x_forward(start, 4, n)
-        x_forward(start + 3, 4, n)
-
-    for c in (corner_down[0], relay_away[0], relay_down[0], pass_top[0], pass_bottom[0]):
-        c.wait_recv()
-    lax.fori_loop(0, 2, near_rows, 0, unroll=2)
-    y_forward_halo(list(range(7, 15)) + list(range(47, 55)))
-    load_rec.wait()
-    lax.fori_loop(1, 3, depth, 0)
+    def edge_rows(start, n):
+        for g in (0, 4, 8, RAD - 4):
+            x_forward(start + g, 4, n)
+
     def y_backward(rows):
         def step(n, c):
             off = pl.ds(pl.multiple_of(n * 8, 8), 8)
@@ -341,20 +326,24 @@
 
         lax.fori_loop(0, 4, step, 0, unroll=4)
 
-    relay_away[1].wait_recv()
-    pass_bottom[1].wait_recv()
-    far_rows(55, 2)
-    y_forward_halo(list(range(55, 62)))
-    depth(3, 0)
+    for c in (*relay_away, *pass_bottom):
+        c.wait_recv()
+    edge_rows(RAD + B, 2)
+    y_forward_halo(list(range(RAD + B, ROWS)))
+    load_rec.wait()
+    lax.fori_loop(2, 4, depth, 0)
     y_backward([range(47, 55), range(55, 62)])
     halo_back(RAD + B, 2)
     sum_away.start()
     mate_bottom.start()
-    for c in (corner_down[1], relay_down[1], pass_top[1]):
+    for n in range(2):
+        edge_down[n].wait_recv()
+        pass_top[n].start()
+    for c in (*corner_down, *relay_down, *pass_top):
         c.wait_recv()
-    far_rows(0, 1)
-    y_forward_halo(list(range(0, 7)))
-    depth(0, 0)
+    edge_rows(0, 1)
+    y_forward_halo(list(range(0, RAD)))
+    lax.fori_loop(0, 2, depth, 0)
     mate_bottom.wait_recv()
     p[bottom, col(H + own_mate), :] += rpc[1]
     back_down.start()

time: 50.3 us -> 49.2 us (0.978)
  the two profiles are of different devices: /device:TPU:1 before, /device:TPU:29 now
where the time goes in v6:
time: 49.2 us; the launch traced here: 49.1 us
  Pallas kernels  47.2 us (96%)
  local copies, waits for them, and re-layouts  1.87 us (4%)
    pallas_call x1, Pallas kernels, body(): pl.pallas_call(functools.partial(kernel, ny, nx), out_shape=jax.ShapeDtyp...  47.2 us
    unnamed x1, local copies, waits for them, and re-layouts  1.87 us

profile of v6, /device:TPU:29, one launch (start us, length us, event | category | flops | bytes accessed | tf_op | source)
XLA Modules:
  0.0 49.1 jit_solution(18437906962515318109)
XLA Ops:
  0.0 47.2 %richardson_lucy.1 = f32[32,32,128]{2,1,0:T(8,128)} custom-call(f32[32,32,128]{2,1,0:T(8,128)} %cur.1, f32[4,32,32,128]{3,2,1,0:T(8,128)} %rec.1, f32[4,31]{1,0:T(4,128)} %kz.1, f32[4,31]{1,0:T(4,128)} %ky.1, f32[4,31]{1,0:T(4,128)} %kx.1), custom_call_target="tpu_custom_call" | custom-call | tf_op jit(solution)/shard_map/richardson_lucy/pallas_call | solution.py:400
  47.2 1.9 %copy.7 = f32[32,32,128]{2,1,0:T(8,128)} copy(f32[32,32,128]{2,1,0:T(8,128)} %richardson_lucy.1) | data formatting | bytes 1048576

commit v7 on v6

--- a/solution.py
+++ b/solution.py
@@ -333,12 +333,12 @@
     load_rec.wait()
     lax.fori_loop(2, 4, depth, 0)
     y_backward([range(47, 55), range(55, 62)])
+    for n in range(2):
+        edge_down[n].wait_recv()
+        pass_top[n].start()
     halo_back(RAD + B, 2)
     sum_away.start()
     mate_bottom.start()
-    for n in range(2):
-        edge_down[n].wait_recv()
-        pass_top[n].start()
     for c in (*corner_down, *relay_down, *pass_top):
         c.wait_recv()
     edge_rows(0, 1)

time: 49.2 us -> 50.5 us (1.026)
  the two profiles are of different devices: /device:TPU:29 before, /device:TPU:1 now
where the time goes in v7:
time: 50.5 us; the launch traced here: 50.3 us
  Pallas kernels  48.4 us (96%)
  local copies, waits for them, and re-layouts  1.87 us (4%)
    pallas_call x1, Pallas kernels, body(): pl.pallas_call(functools.partial(kernel, ny, nx), out_shape=jax.ShapeDtyp...  48.4 us
    unnamed x1, local copies, waits for them, and re-layouts  1.87 us

profile of v7, /device:TPU:1, one launch (start us, length us, event | category | flops | bytes accessed | tf_op | source)
XLA Modules:
  0.0 50.3 jit_solution(6173024581830027124)
XLA Ops:
  0.0 48.4 %richardson_lucy.1 = f32[32,32,128]{2,1,0:T(8,128)} custom-call(f32[32,32,128]{2,1,0:T(8,128)} %cur.1, f32[4,32,32,128]{3,2,1,0:T(8,128)} %rec.1, f32[4,31]{1,0:T(4,128)} %kz.1, f32[4,31]{1,0:T(4,128)} %ky.1, f32[4,31]{1,0:T(4,128)} %kx.1), custom_call_target="tpu_custom_call" | custom-call | tf_op jit(solution)/shard_map/richardson_lucy/pallas_call | solution.py:400
  48.5 1.9 %copy.7 = f32[32,32,128]{2,1,0:T(8,128)} copy(f32[32,32,128]{2,1,0:T(8,128)} %richardson_lucy.1) | data formatting | bytes 1048576
